TPU v7x, 128 devices: a whole 4x4x4 slice. The times are simulated.
128 devices in a mesh: role: 2 (over z_hi), dev: 64 (over z_lo, y, x, core).
Axes of the slice: x: 4, y: 4, z: 4 (z_hi: 2, z_lo: 2; z = z_hi * 2 + z_lo), core: 2. Of those that a mesh axis runs over, the one named last changes fastest.
Arguments:
- queries: bfloat16 [512, 64, 576], P(('role', 'dev')), may hold values from -14 to 14
- latent_cache: bfloat16 [512, 512, 576], P(('role', 'dev')), may hold values from -4 to 4
- cache_lengths: int32 [512], P(('role', 'dev')), may hold values from 1 to 512, 163840 in all
- residual: bfloat16 [512, 7168], P(('role', 'dev')), may hold values from -26 to 26
- expert_ids: int32 [512, 8], P(('role', 'dev')), may hold values from 0 to 15, all different within a row; in each aligned block of 2 rows (0 to 1, 2 to 3, ...) at most 2 rows name the same one
- route_weights: float32 [512, 8], P(('role', 'dev')), may hold values from 0.05 to 0.5
- value_weight: bfloat16 [64, 512, 128], P('dev'), may hold values from -2.5 to 2.5
- w_out: bfloat16 [8192, 7168], P('dev'), may hold values from -0.0625 to 0.0625
- w_gate: bfloat16 [128, 7168, 256], P(('role', 'dev')), may hold values from -0.0625 to 0.0625
- w_up: bfloat16 [128, 7168, 256], P(('role', 'dev')), may hold values from -0.0625 to 0.0625
- w_down: bfloat16 [128, 256, 7168], P(('role', 'dev')), may hold values from -0.125 to 0.125
Outputs:
- layer_out: bfloat16 [512, 7168], P(('role', 'dev'))
Inputs may be any that keep to these rules, and one draw needn't show every extreme that they name: `expert_ids`: in every aligned block of 2 rows no expert is named by more than 2 rows.
All inputs are finite; a program needn't handle non-finite values. No bound on the sum of `cache_lengths` on one device may be relied on, other than what follows from the above.
Results may differ from a plain program's by a relative error of at most 0.006.
Values may be sent and summed in bfloat16 or wider, within the bound.
A program may use at most 128 MiB of HBM per device.

v0:
```python
import math

import jax
import jax.numpy as jnp
from jax import lax
from jax.sharding import PartitionSpec as P

KEY_VALUE_RANK = 512
EXPERTS = 16
MICRO = 2
MB_ROWS = 2
CAP = 2


score_scale = 1.0 / math.sqrt(192.0)


def attend(query, latent_store, length):
    scores = (
        jnp.einsum("nhl,ntl->nht", query, latent_store, preferred_element_type=jnp.float32)
        * score_scale
    )
    living = (
        jnp.arange(latent_store.shape[1], dtype=jnp.int32)[None, None, :] < length[:, None, None]
    )
    scores = jnp.where(living, scores, -jnp.inf)
    highest = jnp.max(scores, -1, keepdims=True)
    raised = jnp.exp(scores - highest)
    chances = (raised / jnp.sum(raised, -1, keepdims=True)).astype(jnp.bfloat16)
    latent_content = latent_store[:, :, :KEY_VALUE_RANK]
    return jnp.einsum(
        "nht,ntk->nhk", chances, latent_content, preferred_element_type=jnp.float32
    ).astype(jnp.bfloat16)


def rms_normed(hidden):
    widened = hidden.astype(jnp.float32)
    return (widened * lax.rsqrt(jnp.mean(widened * widened, -1, keepdims=True) + 1e-06)).astype(
        jnp.bfloat16
    )


def routing(expert_ids, route_weights):
    row_count = expert_ids.shape[0]
    onehot = (expert_ids[:, :, None] == jnp.arange(EXPERTS, dtype=jnp.int32)[None, None, :]).astype(
        jnp.float32
    )
    row_hits = jnp.sum(onehot, 1)
    earlier = (
        jnp.arange(row_count, dtype=jnp.int32)[:, None]
        > jnp.arange(row_count, dtype=jnp.int32)[None, :]
    ).astype(jnp.float32)
    counted = jnp.dot(earlier, row_hits, precision=lax.Precision.HIGHEST)
    slot_index = jnp.sum(onehot * counted[:, None, :], -1)
    slot_onehot = (
        slot_index[:, :, None] == jnp.arange(CAP, dtype=jnp.float32)[None, None, :]
    ).astype(jnp.float32)
    placing = jnp.einsum("rke,rkc->rec", onehot, slot_onehot, precision=lax.Precision.HIGHEST)
    weighting = jnp.einsum(
        "rke,rkc->rec",
        onehot * route_weights[:, :, None],
        slot_onehot,
        precision=lax.Precision.HIGHEST,
    )
    return (placing, weighting)


def local(
    queries,
    latent_cache,
    cache_lengths,
    residual,
    expert_ids,
    route_weights,
    value_weight,
    w_out,
    w_gate,
    w_up,
    w_down,
):
    dev_count = lax.axis_size("dev")
    role_count = lax.axis_size("role")
    devices = role_count * dev_count
    split_count = devices // EXPERTS
    width = residual.shape[1]

    def project_heads(relocated_rows):
        value_per_head = jnp.einsum(
            "ztw,twr->ztr", relocated_rows, value_weight, preferred_element_type=jnp.float32
        ).astype(jnp.bfloat16)
        value_per_head = value_per_head.reshape(relocated_rows.shape[0], -1)

        def term(first_row, row_count):
            return jnp.dot(value_per_head, w_out, preferred_element_type=jnp.float32)

        return term

    results = []
    for micro_index in range(MICRO):
        lower_row = micro_index * MB_ROWS
        upper_row = lower_row + MB_ROWS
        latent_result = attend(
            queries[lower_row:upper_row],
            latent_cache[lower_row:upper_row],
            cache_lengths[lower_row:upper_row],
        )
        relocated_rows = lax.all_to_all(
            latent_result, "dev", split_axis=1, concat_axis=0, tiled=True
        )
        term = project_heads(relocated_rows)
        attended = lax.psum_scatter(
            term(jnp.int32(0), MB_ROWS * lax.axis_size("dev")),
            "dev",
            scatter_dimension=0,
            tiled=True,
        )
        hidden = (residual[lower_row:upper_row].astype(jnp.float32) + attended).astype(jnp.bfloat16)
        route_lower_row = micro_index * MB_ROWS
        route_upper_row = route_lower_row + MB_ROWS
        normed = rms_normed(hidden)
        placing, route_weighting = routing(
            expert_ids[route_lower_row:route_upper_row],
            route_weights[route_lower_row:route_upper_row],
        )
        outgoing = jnp.einsum(
            "rec,rd->ecd", placing.astype(jnp.bfloat16), normed, preferred_element_type=jnp.float32
        ).astype(jnp.bfloat16)
        outgoing, weighting = (jnp.repeat(outgoing, split_count, axis=0), route_weighting)
        arrived = lax.all_to_all(outgoing, ("role", "dev"), split_axis=0, concat_axis=0, tiled=True)
        flattened = arrived.reshape(-1, width)
        gate_act = jnp.dot(flattened, w_gate[0], preferred_element_type=jnp.float32)
        up_act = jnp.dot(flattened, w_up[0], preferred_element_type=jnp.float32)
        activated = (jax.nn.silu(gate_act) * up_act).astype(jnp.bfloat16)
        partial_out = jnp.dot(activated, w_down[0], preferred_element_type=jnp.float32).astype(
            jnp.bfloat16
        )
        returned_rows = lax.all_to_all(
            partial_out.reshape(arrived.shape),
            ("role", "dev"),
            split_axis=0,
            concat_axis=0,
            tiled=True,
        )
        totals = jnp.sum(
            returned_rows.astype(jnp.float32).reshape(EXPERTS, split_count, CAP, width), 1
        )
        mixture = jnp.einsum("rec,ecd->rd", weighting, totals, precision=lax.Precision.HIGHEST)
        results.append((hidden.astype(jnp.float32) + mixture).astype(jnp.bfloat16))
    return jnp.concatenate(results, 0)


def solution(mesh):
    return jax.shard_map(
        local,
        mesh=mesh,
        in_specs=(
            P(("role", "dev"), None, None),
            P(("role", "dev"), None, None),
            P(("role", "dev")),
            P(("role", "dev"), None),
            P(("role", "dev"), None),
            P(("role", "dev"), None),
            P("dev", None, None),
            P("dev", None),
            P(("role", "dev"), None, None),
            P(("role", "dev"), None, None),
            P(("role", "dev"), None, None),
        ),
        out_specs=P(("role", "dev"), None),
        check_vma=False,
    )
```

profile of v0, /device:TPU:0, one launch (start us, length us, event | category | flops | bytes accessed | tf_op | source)
XLA Modules:
  0.0 855.9 jit_solution(6289504029313509908)
XLA Ops:
  11.9 9.4 %all-to-all-start = ((bf16[2,64,512]{2,0,1:T(2,128)(2,1)}), bf16[2,64,512]{2,0,1:T(2,128)(2,1)S(1)}, u32[]{:S(2)}, u32[]{:S(2)}) async-start(bf16[2,64,512]{2,0,1:T(2,128)(2,1)} %copy.23), calls=%async_computation | async-start | bytes 262144 | tf_op jit(solution)/shard_map/all_to_all | solution.py:107
  25.6 4.2 all-to-all-done
  29.8 4.7 all-to-all-start.3
  34.6 8.4 all-to-all-done.3
  51.1 565.3 %all-reduce.5.cloned.1.call-done = (f32[128,7168]{1,0:T(8,128)}, f32[128,7168]{1,0:T(8,128)}) async-done(((f32[128,7168]{1,0:T(8,128)}, f32[128,7168]{1,0:T(8,128)}), (f32[128,7168]{1,0:T(8,128)}, f32[128,7168]{1,0:T(8,128)})) %all-reduce.5.cloned.1.call-update) | async-done | bytes 7340048
  622.3 9.8 %all-to-all-start.1 = ((bf16[128,2,7168]{2,1,0:T(2,128)(2,1)}), bf16[128,2,7168]{2,1,0:T(2,128)(2,1)}, u32[]{:S(2)}, u32[]{:S(2)}) async-start(bf16[128,2,7168]{2,1,0:T(2,128)(2,1)} %bitcast.87), calls=%async_computation.1 | async-start | bytes 7340032 | tf_op jit(solution)/shard_map/all_to_all | solution.py:129
  633.1 45.9 %all-to-all-done.1 = bf16[128,2,7168]{2,1,0:T(2,128)(2,1)} async-done(((bf16[128,2,7168]{2,1,0:T(2,128)(2,1)}), bf16[128,2,7168]{2,1,0:T(2,128)(2,1)}, u32[]{:S(2)}, u32[]{:S(2)}) %all-to-all-start.1) | async-done | bytes 3670048 | tf_op jit(solution)/shard_map/all_to_all | solution.py:129
  679.0 3.8 broadcast_in_dim.26
  682.8 6.2 all-to-all-start.4
  689.0 8.4 reshape.121
  697.4 4.3 fusion.14
  701.7 10.0 %convolution_convert_fusion.1 = bf16[256,7168]{1,0:T(8,128)(2,1)} fusion(bf16[1,256,7168]{2,1,0:T(8,128)(2,1)} %param.21, bf16[256,7168]{1,0:T(8,128)(2,1)} %reshape.121, bf16[1,7168,256]{2,1,0:T(8,128)(2,1)} %param.20, f32[256,256]{1,0:T(8,128)S(1)} %fusion.14), kind=kOutput, calls=%fused_computation.3 | convolution fusion | flops 1881276416 | bytes 14942208 | tf_op jit(solution)/shard_map/dot_general | solution.py:134
  711.7 8.1 reshape.122
  719.8 16.1 %all-to-all-done.4 = bf16[128,2,7168]{2,1,0:T(2,128)(2,1)} async-done(((bf16[128,2,7168]{2,1,0:T(2,128)(2,1)}), bf16[128,2,7168]{2,1,0:T(2,128)(2,1)}, u32[]{:S(2)}, u32[]{:S(2)}) %all-to-all-start.4) | async-done | bytes 3670048 | tf_op jit(solution)/shard_map/all_to_all | solution.py:129
  735.9 5.9 all-to-all-start.2
  741.8 8.4 reshape.127
  750.2 4.3 fusion.12
  754.5 10.0 %convolution_convert_fusion = bf16[256,7168]{1,0:T(8,128)(2,1)} fusion(bf16[1,256,7168]{2,1,0:T(8,128)(2,1)} %param.21, bf16[256,7168]{1,0:T(8,128)(2,1)} %reshape.127, bf16[1,7168,256]{2,1,0:T(8,128)(2,1)} %param.20, f32[256,256]{1,0:T(8,128)S(1)} %fusion.12), kind=kOutput, calls=%fused_computation.2 | convolution fusion | flops 1881276416 | bytes 14942208 | tf_op jit(solution)/shard_map/dot_general | solution.py:134
  764.5 8.1 reshape.128
  772.6 16.1 %all-to-all-done.2 = bf16[128,2,7168]{2,1,0:T(2,128)(2,1)} async-done(((bf16[128,2,7168]{2,1,0:T(2,128)(2,1)}), bf16[128,2,7168]{2,1,0:T(2,128)(2,1)}, u32[]{:S(2)}, u32[]{:S(2)}) %all-to-all-start.2) | async-done | bytes 3670048 | tf_op jit(solution)/shard_map/all_to_all | solution.py:137
  788.7 6.0 all-to-all-start.5
  795.1 5.9 convert_reduce_fusion.1
  801.8 39.8 %all-to-all-done.5 = bf16[128,2,7168]{2,1,0:T(2,128)(2,1)} async-done(((bf16[128,2,7168]{2,1,0:T(2,128)(2,1)}), bf16[128,2,7168]{2,1,0:T(2,128)(2,1)}, u32[]{:S(2)}, u32[]{:S(2)}) %all-to-all-start.5) | async-done | bytes 3670048 | tf_op jit(solution)/shard_map/all_to_all | solution.py:137
  841.6 5.7 convert_reduce_fusion
  (55 shorter events, 26.7 us)
Async XLA Ops:
  6.5 36.5 %copy-start = (bf16[128,7168]{1,0:T(8,128)(2,1)S(1)}, bf16[128,7168]{1,0:T(8,128)(2,1)}, u32[]{:S(2)}) copy-start(bf16[128,7168]{1,0:T(8,128)(2,1)} %param.18) | copy-start | bytes 5505028
  6.5 14.8 %copy-start.6 = (bf16[4,64,576]{2,1,0:T(8,128)(2,1)S(1)}, bf16[4,64,576]{2,1,0:T(8,128)(2,1)}, u32[]{:S(2)}) copy-start(bf16[4,64,576]{2,1,0:T(8,128)(2,1)} %param.11) | copy-start | bytes 884740
  11.1 32.0 %copy-start.2 = (bf16[1,512,128]{2,1,0:T(8,128)(2,1)S(1)}, bf16[1,512,128]{2,1,0:T(8,128)(2,1)}, u32[]{:S(2)}) copy-start(bf16[1,512,128]{2,1,0:T(8,128)(2,1)} %param.17) | copy-start | bytes 393220
  11.9 17.9 %all-to-all-start = ((bf16[2,64,512]{2,0,1:T(2,128)(2,1)}), bf16[2,64,512]{2,0,1:T(2,128)(2,1)S(1)}, u32[]{:S(2)}, u32[]{:S(2)}) async-start(bf16[2,64,512]{2,0,1:T(2,128)(2,1)} %copy.23), calls=%async_computation | async-start | bytes 262144 | tf_op jit(solution)/shard_map/all_to_all | solution.py:107
  29.8 13.2 %all-to-all-start.3 = ((bf16[2,64,512]{2,0,1:T(2,128)(2,1)}), bf16[2,64,512]{2,0,1:T(2,128)(2,1)S(1)}, u32[]{:S(2)}, u32[]{:S(2)}) async-start(bf16[2,64,512]{2,0,1:T(2,128)(2,1)} %copy.29), calls=%async_computation.3 | async-start | bytes 262144 | tf_op jit(solution)/shard_map/all_to_all | solution.py:107
  34.5 581.9 %all-reduce.5.cloned.1.call-start = ((), (), s32[]{:S(2)}) async-start(), calls=%async_computation.6 | async-start | bytes 14680064
  48.4 0.7 copy-start.7
  48.4 1.9 copy-start.4
  48.4 568.0 %copy-start.3 = (bf16[4,7168]{1,0:T(4,128)(2,1)S(1)}, bf16[4,7168]{1,0:T(4,128)(2,1)}, u32[]{:S(2)}) copy-start(bf16[4,7168]{1,0:T(4,128)(2,1)} %param.14) | copy-start | bytes 172036
  622.3 56.7 %all-to-all-start.1 = ((bf16[128,2,7168]{2,1,0:T(2,128)(2,1)}), bf16[128,2,7168]{2,1,0:T(2,128)(2,1)}, u32[]{:S(2)}, u32[]{:S(2)}) async-start(bf16[128,2,7168]{2,1,0:T(2,128)(2,1)} %bitcast.87), calls=%async_computation.1 | async-start | bytes 7340032 | tf_op jit(solution)/shard_map/all_to_all | solution.py:129
  682.8 53.1 %all-to-all-start.4 = ((bf16[128,2,7168]{2,1,0:T(2,128)(2,1)}), bf16[128,2,7168]{2,1,0:T(2,128)(2,1)}, u32[]{:S(2)}, u32[]{:S(2)}) async-start(bf16[128,2,7168]{2,1,0:T(2,128)(2,1)} %bitcast.88), calls=%async_computation.4 | async-start | bytes 7340032 | tf_op jit(solution)/shard_map/all_to_all | solution.py:129
  735.9 52.8 %all-to-all-start.2 = ((bf16[128,2,7168]{2,1,0:T(2,128)(2,1)}), bf16[128,2,7168]{2,1,0:T(2,128)(2,1)}, u32[]{:S(2)}, u32[]{:S(2)}) async-start(bf16[128,2,7168]{2,1,0:T(2,128)(2,1)} %reshape.122), calls=%async_computation.2 | async-start | bytes 7340032 | tf_op jit(solution)/shard_map/all_to_all | solution.py:137
  772.6 22.1 %copy-start.5 = (f32[4,8]{1,0:T(4,128)S(1)}, f32[4,8]{1,0:T(4,128)}, u32[]{:S(2)}) copy-start(f32[4,8]{1,0:T(4,128)} %param.16) | copy-start | bytes 388
  788.7 52.9 %all-to-all-start.5 = ((bf16[128,2,7168]{2,1,0:T(2,128)(2,1)}), bf16[128,2,7168]{2,1,0:T(2,128)(2,1)}, u32[]{:S(2)}, u32[]{:S(2)}) async-start(bf16[128,2,7168]{2,1,0:T(2,128)(2,1)} %reshape.128), calls=%async_computation.5 | async-start | bytes 7340032 | tf_op jit(solution)/shard_map/all_to_all | solution.py:137
  795.1 53.7 %copy-start.1 = (bf16[128,7168]{1,0:T(8,128)(2,1)S(1)}, bf16[128,7168]{1,0:T(8,128)(2,1)}, u32[]{:S(2)}) copy-start(bf16[128,7168]{1,0:T(8,128)(2,1)} %param.18) | copy-start | bytes 5505028
Sparse Core Ops, SparseCore 0:
  48.6 567.7 all-reduce.4
where the time goes:
time: 866 us; the launch traced here: 856 us
  waiting for transfers between devices  696 us (80%)
  local copies, waits for them, and re-layouts  45.3 us (5%)
  matrix products  43.9 us (5%)
  starting transfers between devices  42.1 us (5%)
  between operations  14.5 us (2%)
  other arithmetic  14.4 us (2%)
    unnamed x2, waiting for transfers between devices  565 us
    all_to_all x2, waiting for transfers between devices, local(): lax.all_to_all(outgoing, ('role', 'dev'), split_axis=0, concat_axis=0, ti...  61.9 us
    all_to_all x2, waiting for transfers between devices, local(): lax.all_to_all(partial_out.reshape(arrived.shape), ('role', 'dev'), split...  55.9 us
    dot_general x2, matrix products, local(): jnp.dot(activated, w_down[0], preferred_element_type=jnp.float32)  20 us
  transfers between devices with their start and end apart: 7, of which 7 were waited for; matrix products, arithmetic and copies ran while one was open for 9% of the time, Pallas kernels for 0%

commit v1 on v0

v1 whole, which is shorter than its diff:
```python
import math

import jax
import jax.numpy as jnp
from jax import lax
from jax.experimental import pallas as pl
from jax.experimental.pallas import tpu as pltpu
from jax.sharding import PartitionSpec as P

KEY_VALUE_RANK = 512
EXPERTS = 16
MESH = pl.DeviceIdType.MESH
D = 7168
Q = D // 4
FF = 256
HEAD = 128
BF = jnp.bfloat16
F32 = jnp.float32
score_scale = 1.0 / math.sqrt(192.0)


def attend(query, latent_store, length):
    scores = (
        jnp.einsum("nhl,ntl->nht", query, latent_store, preferred_element_type=jnp.float32)
        * score_scale
    )
    living = (
        jnp.arange(latent_store.shape[1], dtype=jnp.int32)[None, None, :] < length[:, None, None]
    )
    scores = jnp.where(living, scores, -jnp.inf)
    highest = jnp.max(scores, -1, keepdims=True)
    raised = jnp.exp(scores - highest)
    chances = (raised / jnp.sum(raised, -1, keepdims=True)).astype(jnp.bfloat16)
    latent_content = latent_store[:, :, :KEY_VALUE_RANK]
    return jnp.einsum(
        "nht,ntk->nhk", chances, latent_content, preferred_element_type=jnp.float32
    ).astype(jnp.bfloat16)


def parts_of(tiles):
    offset, parts = 0, []
    for count in tiles:
        parts.append((offset * 128, count * 128))
        offset += count
    assert offset * 128 == Q
    return parts


B_PARTS = parts_of((3, 3, 3, 3, 2))
B_BITS = ("x1", "y1", "z0", "x0", "y0")
C_PARTS = parts_of((3, 2, 2, 3, 2, 2))
C_BITS = ("x1", "y1", "z1", "x0", "y0", "z0")
B_DIMS = ("z0", "y1", "y0", "x1", "x0")
C_DIMS = ("z1",) + B_DIMS
T_DIMS = ("z1", "z0", "y1", "y0")
EVERY = slice(None)


class Sems:
    def __init__(self, sends, recvs):
        self.sends, self.recvs, self.count, self.pending = sends, recvs, 0, []

    def remote(self, source, target, landing, device):
        n = self.count
        self.count += 1
        copy = pltpu.make_async_remote_copy(
            src_ref=source,
            dst_ref=target,
            send_sem=self.sends.at[n],
            recv_sem=self.recvs.at[n],
            device_id=device,
            device_id_type=MESH,
        )
        copy.start()
        self.pending.append(copy)
        return pltpu.make_async_remote_copy(
            src_ref=source,
            dst_ref=landing,
            send_sem=self.sends.at[n],
            recv_sem=self.recvs.at[n],
            device_id=device,
            device_id_type=MESH,
        ).wait_recv


SEMS = 136


def kernel(
    rel_ref, res_ref, wts_ref, vw_ref, wo_hbm, wg_hbm, wu_hbm, wd_hbm, out_ref,
    wo, wg, wu, wd, resx, wx, hid, sb, ab, rbc, rb, ss, ssr, tab, g, accg, accu, act,
    sh, ah, rhc, rh, outs, fsend, frecv, loads, sends, recvs,
):
    role, dev = lax.axis_index("role"), lax.axis_index("dev")
    core, x, y, zl = dev % 2, (dev // 2) % 4, (dev // 8) % 4, dev // 32
    own = {
        "x1": x // 2, "x0": (x + x // 2) % 2, "y1": y // 2, "y0": (y + y // 2) % 2,
        "z1": role, "z0": (zl + role) % 2,
    }
    partner = {
        "core": (role, dev + 1 - 2 * core),
        "x1": (role, dev + 2 * (3 - 2 * x)),
        "x0": (role, dev + 2 * (1 - 2 * (x % 2))),
        "xd": (role, dev + 2 * ((x + 2) % 4 - x)),
        "y1": (role, dev + 8 * (3 - 2 * y)),
        "y0": (role, dev + 8 * (1 - 2 * (y % 2))),
        "z1": (1 - role, dev + 32 * (1 - 2 * zl)),
        "z0": (role, dev + 32 * (1 - 2 * zl)),
    }
    sibling = 1 - core

    fetch = []

    def load(source, target):
        copy = pltpu.make_async_copy(source, target, loads.at[len(fetch)])
        copy.start()
        fetch.append(copy)
        return copy

    wo_loads = [load(wo_hbm.at[:, pl.ds(q * Q, Q)], wo.at[q]) for q in range(4)]
    wg_load, wu_load = load(wg_hbm, wg), load(wu_hbm, wu)
    wd_loads = [load(wd_hbm.at[:, pl.ds(q * Q, Q)], wd.at[q]) for q in range(4)]

    barrier = pltpu.get_barrier_semaphore()
    for device in partner.values():
        pl.semaphore_signal(barrier, inc=1, device_id=device, device_id_type=MESH)
    pl.semaphore_wait(barrier, len(partner))

    sems = Sems(sends, recvs)
    x1, x0 = own["x1"], own["x0"]
    lines = (("x0", x1, 1 - x0), ("x1", 1 - x1, x0), ("xd", 1 - x1, 1 - x0))

    arrivals = []
    for name, p1, p0 in lines:
        arrivals.append(sems.remote(res_ref.at[p1, p0], resx.at[x1, x0], resx.at[p1, p0], partner[name]))
        arrivals.append(sems.remote(wts_ref, wx.at[x1, x0], wx.at[p1, p0], partner[name]))
    resx[x1, x0] = res_ref[x1, x0]
    wx[x1, x0] = wts_ref[...]

    for copy in wo_loads:
        copy.wait()

    def project(half, target):
        values = jnp.dot(rel_ref[half], vw_ref[...], preferred_element_type=F32).astype(BF)

        def quarter(q):
            product = jnp.dot(values, wo[q], preferred_element_type=F32).astype(BF)
            target[:, :, :, q // 2, q % 2] = product.reshape(2, 2, 2, 16, Q)

        return quarter

    quarter = project(sibling, sb)
    waits = []
    for q in range(4):
        quarter(q)
        where = (EVERY, EVERY, EVERY, q // 2, q % 2)
        waits.append(sems.remote(sb.at[where], rbc.at[where], rbc.at[where], partner["core"]))
    quarter = project(core, ab)
    for q in range(4):
        quarter(q)
    for q in range(4):
        waits[q]()
        where = (EVERY, EVERY, EVERY, q // 2, q % 2)
        ab[where] = ab[where] + rbc[where]

    def reduce_scatter(buf, landing, dims, bits, parts):
        number = len(bits)
        waits = {}

        def place(k, step, current):
            order = [bits[(k + j) % number] for j in range(number)]
            indices = []
            for dim in dims:
                at = order.index(dim)
                if at < step:
                    indices.append(own[dim])
                elif at == step:
                    indices.append(own[dim] if current else 1 - own[dim])
                else:
                    indices.append(EVERY)
            return tuple(indices) + (EVERY, pl.ds(*parts[k])), order[step]

        for step in range(number):
            for k in range(len(parts)):
                if step:
                    waits[k]()
                    mine, _ = place(k, step - 1, True)
                    other, _ = place(k, step - 1, False)
                    buf[mine] = buf[mine] + landing[other]
                mine, bit = place(k, step, True)
                other, _ = place(k, step, False)
                waits[k] = sems.remote(buf.at[other], landing.at[mine], landing.at[other], partner[bit])
        last = []
        for k in range(len(parts)):
            waits[k]()
            mine, _ = place(k, number - 1, True)
            other, _ = place(k, number - 1, False)
            last.append((parts[k], mine, other))
        return last

    last = reduce_scatter(ab, rb, B_DIMS, B_BITS, B_PARTS)

    for wait in arrivals:
        wait()
    for j in range(4):
        hid[4 * j:4 * j + 4, :] = resx[j // 2, j % 2]
    block = tuple(own[dim] for dim in C_DIMS)
    squares = jnp.zeros((16, 1), F32)
    for (start, width), mine, other in last:
        columns = pl.ds(start, width)
        total = hid[:, columns] + (ab[mine].astype(F32) + rb[other].astype(F32))
        rounded = total.astype(BF)
        g[(core,) + block + (EVERY, columns)] = rounded
        total = rounded.astype(F32)
        hid[:, columns] = total
        squares = squares + jnp.sum(total * total, axis=1, keepdims=True)
    ss[0] = jnp.broadcast_to(squares, (16, 128))

    def gather_place(k, step, mine, bits, dims):
        number = len(bits)
        order = [bits[(k + number - 1 - j) % number] for j in range(number)]
        indices = []
        for dim in dims:
            at = order.index(dim)
            if at < step:
                indices.append(EVERY)
            elif at == step:
                indices.append(own[dim] if mine else 1 - own[dim])
            else:
                indices.append(own[dim])
        return tuple(indices), order[step]

    waits, forwards = {}, []
    table_waits = []
    t_bits = ("y0", "y1", "z0", "z1")
    lanes = lax.broadcasted_iota(jnp.int32, (16, 128), 1)
    steps = len(C_BITS)
    for step in range(steps + 1):
        for k in range(len(C_PARTS)):
            tail = (EVERY, pl.ds(*C_PARTS[k]))
            if step:
                waits[k]()
            if step < steps:
                mine, bit = gather_place(k, step, True, C_BITS, C_DIMS)
                other, _ = gather_place(k, step, False, C_BITS, C_DIMS)
                here = g.at[(core,) + mine + tail]
                waits[k] = sems.remote(here, here, g.at[(core,) + other + tail], partner[bit])
            if step >= steps - 1:
                mine, _ = gather_place(k, steps - 1, step == steps - 1, C_BITS, C_DIMS)
                here = g.at[(core,) + mine + tail]
                forwards.append(sems.remote(here, here, g.at[(sibling,) + mine + tail], partner["core"]))
        if step < 2:
            table_waits.append(sems.remote(ss.at[step], ssr.at[step], ssr.at[step], partner[("x0", "x1")[step]]))
            table_waits[-1]()
            ss[step + 1] = ss[step] + ssr[step]
            if step == 1:
                weights = jnp.concatenate([wx[j // 2, j % 2] for j in range(4)], axis=0)
                scale = lax.rsqrt(ss[2] * (1.0 / D) + 1e-06)
                tab[(core,) + tuple(own[dim] for dim in T_DIMS)] = jnp.where(lanes == EXPERTS, scale, weights)
        elif step < 6:
            if step > 2:
                table_waits[-1]()
            mine, bit = gather_place(3, step - 2, True, t_bits, T_DIMS)
            other, _ = gather_place(3, step - 2, False, t_bits, T_DIMS)
            here = tab.at[(core,) + mine]
            table_waits.append(sems.remote(here, here, tab.at[(core,) + other], partner[bit]))
        else:
            table_waits[-1]()
            table_waits.append(sems.remote(tab.at[core], tab.at[core], tab.at[sibling], partner["core"]))

    wg_load.wait()
    wu_load.wait()
    expert = role * 8 + zl * 4 + y
    rows_lanes = lax.broadcasted_iota(jnp.int32, (256, 128), 1)

    def gate_up(half):
        accg[...] = jnp.zeros_like(accg)
        accu[...] = jnp.zeros_like(accu)

        def quarter(q, carry):
            rows = g[half, :, :, :, :, q // 2, q % 2].reshape(256, Q)
            accg[...] += jnp.dot(rows, wg[q], preferred_element_type=F32)
            accu[...] += jnp.dot(rows, wu[q], preferred_element_type=F32)
            return carry

        lax.fori_loop(0, 4, quarter, 0)

    def activate(half):
        table = tab[half].reshape(256, 128)
        weight = jnp.sum(jnp.where(rows_lanes == expert, table, 0.0), axis=1, keepdims=True)
        scale = jnp.sum(jnp.where(rows_lanes == EXPERTS, table, 0.0), axis=1, keepdims=True)
        gate = accg[...] * scale
        act[half] = (jax.nn.silu(gate) * (accu[...] * scale) * weight).astype(BF)

    gate_up(core)
    activate(core)
    table_waits[-1]()
    for wait in forwards:
        wait()
    gate_up(sibling)
    activate(sibling)
    for copy in wd_loads:
        copy.wait()

    def down(half, target, q):
        for start in range(0, Q, 256):
            product = jnp.dot(act[half], wd[q, :, start:start + 256], preferred_element_type=F32).astype(BF)
            target[:, :, :, :, q // 2, q % 2, :, start:start + 256] = product.reshape(2, 2, 2, 2, 16, 256)

    waits = []
    for q in range(4):
        down(sibling, sh, q)
        where = (EVERY,) * 4 + (q // 2, q % 2)
        waits.append(sems.remote(sh.at[where], rhc.at[where], rhc.at[where], partner["core"]))
    for q in range(4):
        down(core, ah, q)
    for q in range(4):
        waits[q]()
        where = (EVERY,) * 4 + (q // 2, q % 2)
        ah[where] = ah[where] + rhc[where]
    last = reduce_scatter(ah, rh, C_DIMS, C_BITS, C_PARTS)
    for (start, width), mine, other in last:
        columns = pl.ds(start, width)
        outs[:, columns] = hid[:, columns] + (ah[mine].astype(F32) + rh[other].astype(F32))

    for j in range(4):
        fsend[j // 2, j % 2] = outs[4 * j:4 * j + 4, :]
    waits = [
        sems.remote(fsend.at[p1, p0], frecv.at[x1, x0], frecv.at[p1, p0], partner[name])
        for name, p1, p0 in lines
    ]
    frecv[x1, x0] = fsend[x1, x0]
    for wait in waits:
        wait()
    for j in range(4):
        out_ref[:, j * Q:(j + 1) * Q] = frecv[j // 2, j % 2].astype(BF)
    assert sems.count <= SEMS
    for copy in sems.pending:
        copy.wait_send()


def layer(rel, residual, weights, value_weight, w_out, w_gate, w_up, w_down):
    vmem = pl.BlockSpec(memory_space=pltpu.VMEM)
    hbm = pl.BlockSpec(memory_space=pl.ANY)
    b_shape, c_shape = (2,) * 5 + (16, Q), (2,) * 6 + (16, Q)
    return pl.pallas_call(
        kernel,
        out_shape=jax.ShapeDtypeStruct((4, D), BF),
        in_specs=[vmem] * 4 + [hbm] * 4,
        out_specs=vmem,
        scratch_shapes=[
            pltpu.VMEM((4, HEAD, Q), BF),
            pltpu.VMEM((4, Q, FF), BF),
            pltpu.VMEM((4, Q, FF), BF),
            pltpu.VMEM((4, FF, Q), BF),
            pltpu.VMEM((2, 2, 4, Q), F32),
            pltpu.VMEM((2, 2, 4, 128), F32),
            pltpu.VMEM((16, Q), F32),
            pltpu.VMEM(b_shape, BF),
            pltpu.VMEM(b_shape, BF),
            pltpu.VMEM(b_shape, BF),
            pltpu.VMEM(b_shape, BF),
            pltpu.VMEM((3, 16, 128), F32),
            pltpu.VMEM((2, 16, 128), F32),
            pltpu.VMEM((2,) * 5 + (16, 128), F32),
            pltpu.VMEM((2,) + c_shape, BF),
            pltpu.VMEM((256, FF), F32),
            pltpu.VMEM((256, FF), F32),
            pltpu.VMEM((2, 256, FF), BF),
            pltpu.VMEM(c_shape, BF),
            pltpu.VMEM(c_shape, BF),
            pltpu.VMEM(c_shape, BF),
            pltpu.VMEM(c_shape, BF),
            pltpu.VMEM((16, Q), F32),
            pltpu.VMEM((2, 2, 4, Q), F32),
            pltpu.VMEM((2, 2, 4, Q), F32),
            pltpu.SemaphoreType.DMA((10,)),
            pltpu.SemaphoreType.DMA((SEMS,)),
            pltpu.SemaphoreType.DMA((SEMS,)),
        ],
        compiler_params=pltpu.CompilerParams(
            collective_id=0, has_side_effects=True, vmem_limit_bytes=58 * 2**20
        ),
    )(rel, residual, weights, value_weight, w_out, w_gate, w_up, w_down)


def local(
    queries, latent_cache, cache_lengths, residual, expert_ids, route_weights,
    value_weight, w_out, w_gate, w_up, w_down,
):
    role = lax.axis_index("role")
    latents = attend(queries, latent_cache, cache_lengths)
    relocated = lax.all_to_all(latents, "dev", split_axis=1, concat_axis=0, tiled=True)
    by_place = relocated.reshape(2, 4, 4, 2, 4, KEY_VALUE_RANK)
    by_place = jnp.where(role == 0, by_place, by_place[::-1])

    def gray(array, axis):
        picks = [lax.slice_in_dim(array, at, at + 1, axis=axis) for at in (0, 1, 3, 2)]
        return jnp.concatenate(picks, axis)

    by_place = gray(gray(by_place, 1), 2)
    rel = by_place.transpose(3, 0, 1, 2, 4, 5).reshape(2, 128, KEY_VALUE_RANK)
    onehot = expert_ids[:, :, None] == jnp.arange(128, dtype=jnp.int32)[None, None, :]
    weights = jnp.sum(jnp.where(onehot, route_weights[:, :, None], 0.0), 1)
    by_quarter = residual.astype(F32).reshape(4, 2, 2, Q).transpose(1, 2, 0, 3)
    return layer(
        rel, by_quarter, weights, value_weight[0], w_out,
        w_gate.reshape(4, Q, FF), w_up.reshape(4, Q, FF), w_down[0],
    )


def solution(mesh):
    return jax.shard_map(
        local,
        mesh=mesh,
        in_specs=(
            P(("role", "dev"), None, None),
            P(("role", "dev"), None, None),
            P(("role", "dev")),
            P(("role", "dev"), None),
            P(("role", "dev"), None),
            P(("role", "dev"), None),
            P("dev", None, None),
            P("dev", None),
            P(("role", "dev"), None, None),
            P(("role", "dev"), None, None),
            P(("role", "dev"), None, None),
        ),
        out_specs=P(("role", "dev"), None),
        check_vma=False,
    )
```

time: 866 us -> 135 us (0.16); the launches traced: 856 us -> 135 us
  waiting for transfers between devices: 696 us -> 8.42 us
  Pallas kernels: 0 us -> 108 us
  local copies, waits for them, and re-layouts: 45.3 us -> 3.51 us
  matrix products: 43.9 us -> 2.98 us
  starting transfers between devices: 42.1 us -> 9.38 us
  between operations: 14.5 us -> 0.13 us
  other arithmetic: 14.4 us -> 2.89 us
    unnamed x2 -> x0, waiting for transfers between devices: 565 us -> none
    all_to_all x6 -> x1, waiting for transfers between devices: 130 us -> 8.42 us  [local(): lax.all_to_all(latents, 'dev', split_axis=1, concat_axis=0, tiled=True)]
    pallas_call x0 -> x1, Pallas kernels: none -> 108 us  [layer(): pl.pallas_call(kernel, out_shape=jax.ShapeDtypeStruct((4, D), BF), in_spe...]
    dot_general x16 -> x0, matrix products: 37.2 us -> none  [the longest x2 20 us: local(): jnp.dot(activated, w_down[0], preferred_element_type=jnp.float32)]
    all_to_all x6 -> x1, starting transfers between devices: 42 us -> 9.38 us  [local(): lax.all_to_all(latents, 'dev', split_axis=1, concat_axis=0, tiled=True)]
    reshape x4 -> x2, local copies, waits for them, and re-layouts: 33.1 us -> 0.88 us  [the longest x1 0.76 us: local(): rel = by_place.transpose(3, 0, 1, 2, 4, 5).reshape(2, 128, KEY_VALUE_RANK)]
    reduce_sum x6 -> x1, other arithmetic: 13.2 us -> 0.67 us  [local(): weights = jnp.sum(jnp.where(onehot, route_weights[:, :, None], 0.0), 1)]
  transfers between devices with their start and end apart: 7 -> 1, of which waited for: 7 -> 1; matrix products, arithmetic and copies ran while one was open for 9% -> 1% of each run, Pallas kernels for 0% -> 0%
where the time goes in v1:
time: 135 us
  Pallas kernels  108 us (80%)
  starting transfers between devices  9.38 us (7%)
  waiting for transfers between devices  8.42 us (6%)
  local copies, waits for them, and re-layouts  3.51 us (3%)
  matrix products  2.98 us (2%)
  other arithmetic  2.89 us (2%)
    pallas_call x1, Pallas kernels, layer(): pl.pallas_call(kernel, out_shape=jax.ShapeDtypeStruct((4, D), BF), in_spe...  108 us
    all_to_all x1, starting transfers between devices, local(): lax.all_to_all(latents, 'dev', split_axis=1, concat_axis=0, tiled=True)  9.38 us
    all_to_all x1, waiting for transfers between devices, local(): lax.all_to_all(latents, 'dev', split_axis=1, concat_axis=0, tiled=True)  8.42 us
  transfers between devices with their start and end apart: 1, of which 1 were waited for; matrix products, arithmetic and copies ran while one was open for 1% of the time, Pallas kernels for 0%

profile of v1, /device:TPU:0, one launch (start us, length us, event | category | flops | bytes accessed | tf_op | source)
XLA Modules:
  0.0 135.1 jit_solution(8657159420890598059)
XLA Ops:
  0.0 0.0 copy-start
  0.0 0.9 iota_compare_fusion.4
  0.9 0.1 copy-done
  1.0 2.2 %fusion.5 = f32[4,64,512]{2,1,0:T(8,128)S(1)} fusion(bf16[4,64,576]{2,1,0:T(8,128)(2,1)S(1)} %copy-done, bf16[4,512,576]{1,2,0:T(8,128)(2,1)} %param.12, pred[4,512]{1,0:T(4,128)(4,1)S(1)} %iota_compare_fusion.4), kind=kOutput, calls=%fused_computation.6 | convolution fusion | flops 151257088 | bytes 3180544 | tf_op jit(solution)/shard_map/nhl,ntl->nht/dot_general | solution.py:24
  3.2 0.2 fusion.21
  3.4 0.0 copy-done.1
  3.4 0.0 copy-start.2
  3.5 0.0 copy-start.3
  3.5 0.0 copy-start.4
  3.5 0.8 fusion.6
  4.2 0.9 copy.20
  5.1 9.4 %all-to-all-start = ((bf16[4,64,512]{2,0,1:T(4,128)(2,1)}), bf16[4,64,512]{2,0,1:T(4,128)(2,1)S(1)}, u32[]{:S(2)}, u32[]{:S(2)}) async-start(bf16[4,64,512]{2,0,1:T(4,128)(2,1)} %copy.20), calls=%async_computation | async-start | bytes 524288 | tf_op jit(solution)/shard_map/all_to_all | solution.py:393
  14.5 0.0 copy-done.2
  14.5 0.7 convert_bitcast_fusion.res_ref
  15.2 0.7 select_reduce_fusion.wts_ref
  15.9 8.4 %all-to-all-done = bf16[4,64,512]{2,0,1:T(4,128)(2,1)S(1)} async-done(((bf16[4,64,512]{2,0,1:T(4,128)(2,1)}), bf16[4,64,512]{2,0,1:T(4,128)(2,1)S(1)}, u32[]{:S(2)}, u32[]{:S(2)}) %all-to-all-start) | async-done | bytes 262176 | tf_op jit(solution)/shard_map/all_to_all | solution.py:393
  24.3 0.1 copy.22
  24.4 0.1 reverse_select_fusion
  24.7 0.2 pad_maximum_fusion
  24.9 0.1 slice.35
  24.9 0.1 fusion.18
  25.1 0.8 reshape.43.rel_ref
  25.8 107.8 %shard_map.109 = bf16[4,7168]{1,0:T(4,128)(2,1)} custom-call(bf16[2,128,512]{2,1,0:T(8,128)(2,1)} %reshape.43.rel_ref, f32[2,2,4,1792]{3,2,1,0:T(4,128)} %convert_bitcast_fusion.res_ref, f32[4,128]{1,0:T(4,128)} %select_reduce_fusion.wts_ref, bf16[512,128]{1,0:T(8,128)(2,1)} %bitcast.23, bf16[128,7168]{1,0:T(8,128)(2,1)} %wo_hbm.1, ...), custom_call_target="tpu_custom_call" | custom-call | tf_op jit(solution)/shard_map/pallas_call | solution.py:346
  133.6 1.5 %copy.25 = bf16[4,7168]{1,0:T(4,128)(2,1)} copy(bf16[4,7168]{1,0:T(4,128)(2,1)} %shard_map.109) | data formatting | bytes 114688
  (5 shorter events, 0.1 us)
Async XLA Ops:
  0.0 1.0 copy-start
  0.0 3.4 %copy-start.1 = (bf16[4,512,576]{1,2,0:T(8,128)(2,1)S(1)}, bf16[4,512,576]{1,2,0:T(8,128)(2,1)}, u32[]{:S(2)}) copy-start(bf16[4,512,576]{1,2,0:T(8,128)(2,1)} %param.12) | copy-start | bytes 7077892
  3.4 11.1 %copy-start.2 = (bf16[4,7168]{1,0:T(4,128)(2,1)S(1)}, bf16[4,7168]{1,0:T(4,128)(2,1)}, u32[]{:S(2)}) copy-start(bf16[4,7168]{1,0:T(4,128)(2,1)} %param.14) | copy-start | bytes 172036
  3.5 11.8 %copy-start.3 = (f32[4,8]{1,0:T(4,128)S(1)}, f32[4,8]{1,0:T(4,128)}, u32[]{:S(2)}) copy-start(f32[4,8]{1,0:T(4,128)} %param.16) | copy-start | bytes 388
  3.5 11.7 %copy-start.4 = (s32[4,8]{1,0:T(4,128)S(1)}, s32[4,8]{1,0:T(4,128)}, u32[]{:S(2)}) copy-start(s32[4,8]{1,0:T(4,128)} %param.15) | copy-start | bytes 388
  5.1 19.2 %all-to-all-start = ((bf16[4,64,512]{2,0,1:T(4,128)(2,1)}), bf16[4,64,512]{2,0,1:T(4,128)(2,1)S(1)}, u32[]{:S(2)}, u32[]{:S(2)}) async-start(bf16[4,64,512]{2,0,1:T(4,128)(2,1)} %copy.20), calls=%async_computation | async-start | bytes 524288 | tf_op jit(solution)/shard_map/all_to_all | solution.py:393

commit v2 on v1

--- a/solution.py
+++ b/solution.py
@@ -8,6 +8,9 @@
 from jax.sharding import PartitionSpec as P
 
 KEY_VALUE_RANK = 512
+HEADS = 64
+LEN = 512
+LATENT = 576
 EXPERTS = 16
 MESH = pl.DeviceIdType.MESH
 D = 7168
@@ -17,24 +20,6 @@
 BF = jnp.bfloat16
 F32 = jnp.float32
 score_scale = 1.0 / math.sqrt(192.0)
-
-
-def attend(query, latent_store, length):
-    scores = (
-        jnp.einsum("nhl,ntl->nht", query, latent_store, preferred_element_type=jnp.float32)
-        * score_scale
-    )
-    living = (
-        jnp.arange(latent_store.shape[1], dtype=jnp.int32)[None, None, :] < length[:, None, None]
-    )
-    scores = jnp.where(living, scores, -jnp.inf)
-    highest = jnp.max(scores, -1, keepdims=True)
-    raised = jnp.exp(scores - highest)
-    chances = (raised / jnp.sum(raised, -1, keepdims=True)).astype(jnp.bfloat16)
-    latent_content = latent_store[:, :, :KEY_VALUE_RANK]
-    return jnp.einsum(
-        "nht,ntk->nhk", chances, latent_content, preferred_element_type=jnp.float32
-    ).astype(jnp.bfloat16)
 
 
 def parts_of(tiles):
@@ -87,8 +72,8 @@
 
 
 def kernel(
-    rel_ref, res_ref, wts_ref, vw_ref, wo_hbm, wg_hbm, wu_hbm, wd_hbm, out_ref,
-    wo, wg, wu, wd, resx, wx, hid, sb, ab, rbc, rb, ss, ssr, tab, g, accg, accu, act,
+    len_ref, res_ref, ids_ref, rw_ref, vw_ref, q_hbm, cache_hbm, wo_hbm, wg_hbm, wu_hbm, wd_hbm, out_ref,
+    qv, cv, lat, mbuf, lbuf, rel, resq, wts, a2a, wo, wg, wu, wd, resx, wx, hid, sb, ab, rbc, rb, ss, ssr, tab, g, accg, accu, act,
     sh, ah, rhc, rh, outs, fsend, frecv, loads, sends, recvs,
 ):
     role, dev = lax.axis_index("role"), lax.axis_index("dev")
@@ -117,14 +102,64 @@
         fetch.append(copy)
         return copy
 
+    attention_loads = [(load(q_hbm.at[n], qv.at[n]), load(cache_hbm.at[n], cv.at[n])) for n in range(4)]
     wo_loads = [load(wo_hbm.at[:, pl.ds(q * Q, Q)], wo.at[q]) for q in range(4)]
     wg_load, wu_load = load(wg_hbm, wg), load(wu_hbm, wu)
     wd_loads = [load(wd_hbm.at[:, pl.ds(q * Q, Q)], wd.at[q]) for q in range(4)]
 
     barrier = pltpu.get_barrier_semaphore()
-    for device in partner.values():
-        pl.semaphore_signal(barrier, inc=1, device_id=device, device_id_type=MESH)
-    pl.semaphore_wait(barrier, len(partner))
+
+    def greet(d, carry):
+        pl.semaphore_signal(barrier, inc=1, device_id=(role, (dev + d) % HEADS), device_id_type=MESH)
+        return carry
+
+    lax.fori_loop(1, HEADS, greet, 0)
+    pl.semaphore_signal(barrier, inc=1, device_id=partner["z1"], device_id_type=MESH)
+
+    for q in range(4):
+        resq[q // 2, q % 2] = res_ref[:, q * Q:(q + 1) * Q].astype(F32)
+    four_lanes = lax.broadcasted_iota(jnp.int32, (4, 128), 1)
+    dense = jnp.zeros((4, 128), F32)
+    for k in range(8):
+        dense = dense + jnp.where(four_lanes == ids_ref[:, k:k + 1], rw_ref[:, k:k + 1], 0.0)
+    wts[...] = dense
+
+    slots = lax.broadcasted_iota(jnp.int32, (HEADS, LEN), 1)
+    for n in range(4):
+        for copy in attention_loads[n]:
+            copy.wait()
+        scores = lax.dot_general(
+            qv[n], cv[n], (((1,), (1,)), ((), ())), preferred_element_type=F32
+        ) * score_scale
+        scores = jnp.where(slots < len_ref[n], scores, -jnp.inf)
+        raised = jnp.exp(scores - jnp.max(scores, axis=1, keepdims=True))
+        chances = (raised / jnp.sum(raised, axis=1, keepdims=True)).astype(BF)
+        lat[n] = jnp.dot(chances, cv[n, :, :KEY_VALUE_RANK], preferred_element_type=F32).astype(BF)
+
+    to = lax.broadcasted_iota(jnp.int32, (256, 256), 0)
+    source = lax.broadcasted_iota(jnp.int32, (256, 256), 1)
+    regroup = jnp.where(source == (to % 16) * 16 + to // 16, 1.0, 0.0).astype(BF)
+    for group in range(4):
+        heads = slice(16 * group, 16 * group + 16)
+        pieces = [lat[n, heads, 128 * c:128 * c + 128] for c in range(4) for n in range(4)]
+        moved = jnp.dot(regroup, jnp.concatenate(pieces, axis=0), preferred_element_type=F32)
+        mbuf[heads] = moved.astype(BF).reshape(16, 16, 128)
+
+    pl.semaphore_wait(barrier, HEADS)
+    seat = (((core * 2 + own["z0"]) * 2 + own["y1"]) * 2 + own["y0"]) * 4 + own["x1"] * 2 + own["x0"]
+
+    def message(head):
+        return pltpu.make_async_remote_copy(
+            src_ref=mbuf.at[head], dst_ref=lbuf.at[seat], send_sem=a2a.at[0], recv_sem=a2a.at[1],
+            device_id=(role, head), device_id_type=MESH,
+        )
+
+    def post(d, carry):
+        message((dev + d) % HEADS).start()
+        return carry
+
+    lax.fori_loop(1, HEADS, post, 0)
+    lbuf[seat] = mbuf[dev]
 
     sems = Sems(sends, recvs)
     x1, x0 = own["x1"], own["x0"]
@@ -132,16 +167,28 @@
 
     arrivals = []
     for name, p1, p0 in lines:
-        arrivals.append(sems.remote(res_ref.at[p1, p0], resx.at[x1, x0], resx.at[p1, p0], partner[name]))
-        arrivals.append(sems.remote(wts_ref, wx.at[x1, x0], wx.at[p1, p0], partner[name]))
-    resx[x1, x0] = res_ref[x1, x0]
-    wx[x1, x0] = wts_ref[...]
+        arrivals.append(sems.remote(resq.at[p1, p0], resx.at[x1, x0], resx.at[p1, p0], partner[name]))
+        arrivals.append(sems.remote(wts, wx.at[x1, x0], wx.at[p1, p0], partner[name]))
+    resx[x1, x0] = resq[x1, x0]
+    wx[x1, x0] = wts[...]
+
+    spread = jnp.where(source == ((to % 64) // 4) * 16 + (to // 64) * 4 + to % 4, 1.0, 0.0).astype(BF)
+    everyone = pltpu.make_async_remote_copy(
+        src_ref=mbuf.at[pl.ds(0, HEADS - 1)], dst_ref=lbuf.at[pl.ds(0, HEADS - 1)],
+        send_sem=a2a.at[0], recv_sem=a2a.at[1], device_id=partner["core"], device_id_type=MESH,
+    )
+    everyone.wait_recv()
+    for group in range(4):
+        rows = lbuf[16 * group:16 * group + 16].reshape(256, 128)
+        moved = jnp.dot(spread, rows, preferred_element_type=F32).astype(BF)
+        for c in range(4):
+            rel[group // 2, 64 * (group % 2):64 * (group % 2) + 64, 128 * c:128 * c + 128] = moved[64 * c:64 * c + 64]
 
     for copy in wo_loads:
         copy.wait()
 
     def project(half, target):
-        values = jnp.dot(rel_ref[half], vw_ref[...], preferred_element_type=F32).astype(BF)
+        values = jnp.dot(rel[half], vw_ref[...], preferred_element_type=F32).astype(BF)
 
         def quarter(q):
             product = jnp.dot(values, wo[q], preferred_element_type=F32).astype(BF)
@@ -335,20 +382,30 @@
     for j in range(4):
         out_ref[:, j * Q:(j + 1) * Q] = frecv[j // 2, j % 2].astype(BF)
     assert sems.count <= SEMS
+    everyone.wait_send()
     for copy in sems.pending:
         copy.wait_send()
 
 
-def layer(rel, residual, weights, value_weight, w_out, w_gate, w_up, w_down):
+def layer(*operands):
     vmem = pl.BlockSpec(memory_space=pltpu.VMEM)
     hbm = pl.BlockSpec(memory_space=pl.ANY)
     b_shape, c_shape = (2,) * 5 + (16, Q), (2,) * 6 + (16, Q)
     return pl.pallas_call(
         kernel,
         out_shape=jax.ShapeDtypeStruct((4, D), BF),
-        in_specs=[vmem] * 4 + [hbm] * 4,
+        in_specs=[pl.BlockSpec(memory_space=pltpu.SMEM)] + [vmem] * 4 + [hbm] * 6,
         out_specs=vmem,
         scratch_shapes=[
+            pltpu.VMEM((4, HEADS, LATENT), BF),
+            pltpu.VMEM((4, LEN, LATENT), BF),
+            pltpu.VMEM((4, HEADS, KEY_VALUE_RANK), BF),
+            pltpu.VMEM((HEADS, 16, 128), BF),
+            pltpu.VMEM((HEADS, 16, 128), BF),
+            pltpu.VMEM((2, 128, KEY_VALUE_RANK), BF),
+            pltpu.VMEM((2, 2, 4, Q), F32),
+            pltpu.VMEM((4, 128), F32),
+            pltpu.SemaphoreType.DMA((2,)),
             pltpu.VMEM((4, HEAD, Q), BF),
             pltpu.VMEM((4, Q, FF), BF),
             pltpu.VMEM((4, Q, FF), BF),
@@ -374,37 +431,22 @@
             pltpu.VMEM((16, Q), F32),
             pltpu.VMEM((2, 2, 4, Q), F32),
             pltpu.VMEM((2, 2, 4, Q), F32),
-            pltpu.SemaphoreType.DMA((10,)),
+            pltpu.SemaphoreType.DMA((18,)),
             pltpu.SemaphoreType.DMA((SEMS,)),
             pltpu.SemaphoreType.DMA((SEMS,)),
         ],
         compiler_params=pltpu.CompilerParams(
             collective_id=0, has_side_effects=True, vmem_limit_bytes=58 * 2**20
         ),
-    )(rel, residual, weights, value_weight, w_out, w_gate, w_up, w_down)
+    )(*operands)
 
 
 def local(
     queries, latent_cache, cache_lengths, residual, expert_ids, route_weights,
     value_weight, w_out, w_gate, w_up, w_down,
 ):
-    role = lax.axis_index("role")
-    latents = attend(queries, latent_cache, cache_lengths)
-    relocated = lax.all_to_all(latents, "dev", split_axis=1, concat_axis=0, tiled=True)
-    by_place = relocated.reshape(2, 4, 4, 2, 4, KEY_VALUE_RANK)
-    by_place = jnp.where(role == 0, by_place, by_place[::-1])
-
-    def gray(array, axis):
-        picks = [lax.slice_in_dim(array, at, at + 1, axis=axis) for at in (0, 1, 3, 2)]
-        return jnp.concatenate(picks, axis)
-
-    by_place = gray(gray(by_place, 1), 2)
-    rel = by_place.transpose(3, 0, 1, 2, 4, 5).reshape(2, 128, KEY_VALUE_RANK)
-    onehot = expert_ids[:, :, None] == jnp.arange(128, dtype=jnp.int32)[None, None, :]
-    weights = jnp.sum(jnp.where(onehot, route_weights[:, :, None], 0.0), 1)
-    by_quarter = residual.astype(F32).reshape(4, 2, 2, Q).transpose(1, 2, 0, 3)
     return layer(
-        rel, by_quarter, weights, value_weight[0], w_out,
+        cache_lengths, residual, expert_ids, route_weights, value_weight[0], queries, latent_cache, w_out,
         w_gate.reshape(4, Q, FF), w_up.reshape(4, Q, FF), w_down[0],
     )
 

time: 135 us -> 127 us (0.941)
  Pallas kernels: 108 us -> 121 us
  starting transfers between devices: 9.38 us -> 0 us
  waiting for transfers between devices: 8.42 us -> 0 us
  matrix products: 2.98 us -> 0 us
  other arithmetic: 2.89 us -> 0 us
  local copies, waits for them, and re-layouts: 3.51 us -> 5.79 us
    pallas_call x1, Pallas kernels: 108 us -> 121 us  [layer(): pl.pallas_call(kernel, out_shape=jax.ShapeDtypeStruct((4, D), BF), in_spe...]
    all_to_all x1 -> x0, starting transfers between devices: 9.38 us -> none  [local(): lax.all_to_all(latents, 'dev', split_axis=1, concat_axis=0, tiled=True)]
    all_to_all x1 -> x0, waiting for transfers between devices: 8.42 us -> none  [local(): lax.all_to_all(latents, 'dev', split_axis=1, concat_axis=0, tiled=True)]
    unnamed x11 -> x2, local copies, waits for them, and re-layouts: 1.58 us -> 5.79 us
    dot_general x2 -> x0, matrix products: 2.98 us -> none  [the longest x1 2.21 us: attend(): jnp.einsum('nhl,ntl->nht', query, latent_store, preferred_element_type=jn...]
  transfers between devices with their start and end apart: 1 -> 0, of which waited for: 1 -> 0; matrix products, arithmetic and copies ran while one was open for 1% -> 0% of each run, Pallas kernels for 0% -> 0%
where the time goes in v2:
time: 127 us
  Pallas kernels  121 us (95%)
  local copies, waits for them, and re-layouts  5.79 us (5%)
    pallas_call x1, Pallas kernels, layer(): pl.pallas_call(kernel, out_shape=jax.ShapeDtypeStruct((4, D), BF), in_spe...  121 us
    unnamed x2, local copies, waits for them, and re-layouts  5.79 us

profile of v2, /device:TPU:0, one launch (start us, length us, event | category | flops | bytes accessed | tf_op | source)
XLA Modules:
  0.0 126.6 jit_solution(191160461252006079)
XLA Ops:
  0.0 4.3 %copy.12.cache_hbm = bf16[4,512,576]{2,1,0:T(8,128)(2,1)} copy(bf16[4,512,576]{1,2,0:T(8,128)(2,1)} %param.12) | data formatting | bytes 4718592 | tf_op args[1]
  4.3 120.8 %shard_map.109 = bf16[4,7168]{1,0:T(4,128)(2,1)} custom-call(s32[4]{0:T(128)} %len_ref.1, bf16[4,7168]{1,0:T(4,128)(2,1)} %res_ref.1, s32[4,8]{1,0:T(4,128)} %ids_ref.1, f32[4,8]{1,0:T(4,128)} %rw_ref.1, bf16[512,128]{1,0:T(8,128)(2,1)} %bitcast.7, bf16[4,64,576]{2,1,0:T(8,128)(2,1)} %q_hbm.1, bf16[4,512,576]{2,1,0:T(8,128)(2,1)} %copy.12.cache_hbm, ...), custom_call_target="tpu_custom_call" | custom-call | tf_op jit(solution)/shard_map/pallas_call | solution.py:394
  125.1 1.5 %copy.14 = bf16[4,7168]{1,0:T(4,128)(2,1)} copy(bf16[4,7168]{1,0:T(4,128)(2,1)} %shard_map.109) | data formatting | bytes 114688

commit v3 on v2

v3 whole, which is shorter than its diff:
```python
import math

import jax
import jax.numpy as jnp
from jax import lax
from jax.experimental import pallas as pl
from jax.experimental.pallas import tpu as pltpu
from jax.sharding import PartitionSpec as P

KEY_VALUE_RANK = 512
HEADS = 64
LEN = 512
LATENT = 576
EXPERTS = 16
MESH = pl.DeviceIdType.MESH
D = 7168
Q = D // 4
FF = 256
HEAD = 128
BF = jnp.bfloat16
F32 = jnp.float32
score_scale = 1.0 / math.sqrt(192.0)


B_DIMS = ("z0", "y1", "y0", "x1", "x0")
C_DIMS = ("z1",) + B_DIMS
HALF = Q // 2
B_GROUPS = ((("x1", "y1"), ("x0", "y0", "z0")), (("x0", "y0"), ("x1", "y1", "z0")))
B_PIECES = ((0, 2, 0), (4, 2, 1), (2, 2, 0), (6, 1, 1))
C_GROUPS = ((("x1", "y1", "z1"), ("x0", "y0", "z0")), (("x0", "y0", "z0"), ("x1", "y1", "z1")))
C_PIECES = ((0, 2, 0), (3, 1, 1), (5, 1, 2), (2, 1, 0), (4, 1, 1), (6, 1, 2))


def all_pieces(groups, pieces):
    found = []
    for tile, count, turn in pieces:
        for at, (ring, _) in enumerate(groups):
            columns = pl.ds(at * HALF + tile * 128, count * 128)
            found.append((at, columns, ring[turn:] + ring[:turn]))
    return found


def subsets(bits):
    found = [tuple(bit for i, bit in enumerate(bits) if n >> i & 1) for n in range(1, 2 ** len(bits))]
    return sorted(found, key=lambda flips: -len(flips))


EVERY = slice(None)


class Sems:
    def __init__(self, sends, recvs):
        self.sends, self.recvs, self.count, self.pending = sends, recvs, 0, []

    def remote(self, source, target, landing, device):
        n = self.count
        self.count += 1
        copy = pltpu.make_async_remote_copy(
            src_ref=source,
            dst_ref=target,
            send_sem=self.sends.at[n],
            recv_sem=self.recvs.at[n],
            device_id=device,
            device_id_type=MESH,
        )
        copy.start()
        self.pending.append(copy)
        return pltpu.make_async_remote_copy(
            src_ref=source,
            dst_ref=landing,
            send_sem=self.sends.at[n],
            recv_sem=self.recvs.at[n],
            device_id=device,
            device_id_type=MESH,
        ).wait_recv


SEMS = 200


def kernel(
    len_ref, res_ref, ids_ref, rw_ref, vw_ref, q_hbm, cache_hbm, wo_hbm, wg_hbm, wu_hbm, wd_hbm, out_ref,
    qv, cv, lat, mbuf, lbuf, rel, resq, wts, a2a, wo, wg, wu, wd, resx, wx, hid, values, sb, ab, rbc, rb, ss, ssr, tab, g, accg, accu, act,
    sh, ah, rhc, rh, outs, fsend, frecv, loads, sends, recvs,
):
    role, dev = lax.axis_index("role"), lax.axis_index("dev")
    core, x, y, zl = dev % 2, (dev // 2) % 4, (dev // 8) % 4, dev // 32
    own = {
        "x1": x // 2, "x0": (x + x // 2) % 2, "y1": y // 2, "y0": (y + y // 2) % 2,
        "z1": role, "z0": (zl + role) % 2,
    }
    def across(*flips):
        at = {bit: 1 - own[bit] if bit in flips else own[bit] for bit in own}
        to_x = 2 * at["x1"] + (at["x1"] + at["x0"]) % 2
        to_y = 2 * at["y1"] + (at["y1"] + at["y0"]) % 2
        to_zl = (at["z1"] + at["z0"]) % 2
        return at["z1"], ((to_zl * 4 + to_y) * 4 + to_x) * 2 + core

    twin = (role, dev + 1 - 2 * core)
    sibling = 1 - core

    fetch = []

    def load(source, target):
        copy = pltpu.make_async_copy(source, target, loads.at[len(fetch)])
        copy.start()
        fetch.append(copy)
        return copy

    attention_loads = [(load(q_hbm.at[n], qv.at[n]), load(cache_hbm.at[n], cv.at[n])) for n in range(4)]
    wo_loads = [load(wo_hbm.at[:, pl.ds(q * Q, Q)], wo.at[q]) for q in range(4)]
    wg_load, wu_load = load(wg_hbm, wg), load(wu_hbm, wu)
    wd_loads = [load(wd_hbm.at[:, pl.ds(q * Q, Q)], wd.at[q]) for q in range(4)]

    barrier = pltpu.get_barrier_semaphore()

    def greet(d, carry):
        pl.semaphore_signal(barrier, inc=1, device_id=(role, (dev + d) % HEADS), device_id_type=MESH)
        return carry

    lax.fori_loop(1, HEADS, greet, 0)
    beyond = [across(*flips) for flips in subsets(("x1", "y1", "z1")) if "z1" in flips]
    for device in beyond:
        pl.semaphore_signal(barrier, inc=1, device_id=device, device_id_type=MESH)

    for q in range(4):
        resq[q // 2, q % 2] = res_ref[:, q * Q:(q + 1) * Q].astype(F32)
    four_lanes = lax.broadcasted_iota(jnp.int32, (4, 128), 1)
    dense = jnp.zeros((4, 128), F32)
    for k in range(8):
        dense = dense + jnp.where(four_lanes == ids_ref[:, k:k + 1], rw_ref[:, k:k + 1], 0.0)
    wts[...] = dense

    slots = lax.broadcasted_iota(jnp.int32, (HEADS, LEN), 1)
    for pair in attention_loads:
        for copy in pair:
            copy.wait()
    scores = [jnp.dot(qv[n], cv[n], preferred_element_type=F32) * score_scale for n in range(4)]
    for n in range(4):
        live = jnp.where(slots < len_ref[n], scores[n], -jnp.inf)
        raised = jnp.exp(live - jnp.max(live, axis=1, keepdims=True))
        chances = (raised / jnp.sum(raised, axis=1, keepdims=True)).astype(BF)
        lat[n] = lax.dot_general(
            chances, cv[n, :KEY_VALUE_RANK, :], (((1,), (1,)), ((), ())), preferred_element_type=F32
        ).astype(BF)

    to = lax.broadcasted_iota(jnp.int32, (256, 256), 0)
    source = lax.broadcasted_iota(jnp.int32, (256, 256), 1)
    regroup = jnp.where(source == (to % 16) * 16 + to // 16, 1.0, 0.0).astype(BF)
    for group in range(4):
        heads = slice(16 * group, 16 * group + 16)
        pieces = [lat[n, heads, 128 * c:128 * c + 128] for c in range(4) for n in range(4)]
        moved = jnp.dot(regroup, jnp.concatenate(pieces, axis=0), preferred_element_type=F32)
        mbuf[heads] = moved.astype(BF).reshape(16, 16, 128)

    pl.semaphore_wait(barrier, HEADS - 1 + len(beyond))
    seat = (((core * 2 + own["z0"]) * 2 + own["y1"]) * 2 + own["y0"]) * 4 + own["x1"] * 2 + own["x0"]

    def message(head):
        return pltpu.make_async_remote_copy(
            src_ref=mbuf.at[head], dst_ref=lbuf.at[seat], send_sem=a2a.at[0], recv_sem=a2a.at[1],
            device_id=(role, head), device_id_type=MESH,
        )

    def post(d, carry):
        message((dev + d) % HEADS).start()
        return carry

    lax.fori_loop(1, HEADS, post, 0)
    lbuf[seat] = mbuf[dev]

    sems = Sems(sends, recvs)
    x1, x0 = own["x1"], own["x0"]
    lines = (
        (across("x1", "x0"), 1 - x1, 1 - x0), (across("x1"), 1 - x1, x0), (across("x0"), x1, 1 - x0),
    )

    arrivals = []
    for device, p1, p0 in lines:
        arrivals.append(sems.remote(resq.at[p1, p0], resx.at[x1, x0], resx.at[p1, p0], device))
        arrivals.append(sems.remote(wts, wx.at[x1, x0], wx.at[p1, p0], device))
    resx[x1, x0] = resq[x1, x0]
    wx[x1, x0] = wts[...]

    spread = jnp.where(source == ((to % 64) // 4) * 16 + (to // 64) * 4 + to % 4, 1.0, 0.0).astype(BF)
    everyone = pltpu.make_async_remote_copy(
        src_ref=mbuf.at[pl.ds(0, HEADS - 1)], dst_ref=lbuf.at[pl.ds(0, HEADS - 1)],
        send_sem=a2a.at[0], recv_sem=a2a.at[1], device_id=twin, device_id_type=MESH,
    )
    everyone.wait_recv()
    for group in range(4):
        rows = lbuf[16 * group:16 * group + 16].reshape(256, 128)
        moved = jnp.dot(spread, rows, preferred_element_type=F32).astype(BF)
        for c in range(4):
            rel[group // 2, 64 * (group % 2):64 * (group % 2) + 64, 128 * c:128 * c + 128] = moved[64 * c:64 * c + 64]

    def reduce_scatter(produce, given, taken, buf, landing, dims, groups, pieces):
        whole = (EVERY,) * (len(dims) + 1)
        found = all_pieces(groups, pieces)
        waits = [None] * len(found)

        def place(order, step, mine):
            indices = []
            for dim in dims:
                at = order.index(dim) if dim in order else len(order)
                here = own[dim] if mine else 1 - own[dim]
                indices.append(own[dim] if at < step else here if at == step else EVERY)
            return tuple(indices) + (EVERY,)

        def advance(n, step):
            _, columns, order = found[n]
            mine, other = place(order, step, True) + (columns,), place(order, step, False) + (columns,)
            if step < len(order):
                waits[n] = sems.remote(buf.at[other], landing.at[mine], landing.at[other], across(order[step]))

        def add(n, step):
            _, columns, order = found[n]
            waits[n]()
            if step < 0:
                buf[whole + (columns,)] = buf[whole + (columns,)] + taken[whole + (columns,)]
            else:
                mine, other = place(order, step, True) + (columns,), place(order, step, False) + (columns,)
                buf[mine] = buf[mine] + landing[other]

        for n, (_, columns, _) in enumerate(found):
            produce(sibling, given, columns)
            where = whole + (columns,)
            waits[n] = sems.remote(given.at[where], taken.at[where], taken.at[where], twin)
            produce(core, buf, columns)
            if n:
                add(n - 1, -1)
                advance(n - 1, 0)
        add(len(found) - 1, -1)
        advance(len(found) - 1, 0)
        rounds = len(groups[0][0])
        for step in range(1, rounds):
            for n in range(len(found)):
                add(n, step - 1)
                advance(n, step)
        result, last = [], []
        for at, (ring, direct) in enumerate(groups):
            columns = pl.ds(at * HALF, HALF)
            for n in range(len(found)):
                if found[n][0] == at:
                    add(n, rounds - 1)
            mine = tuple(own[dim] for dim in dims) + (EVERY, columns)
            others = []
            for flips in subsets(direct):
                other = tuple(1 - own[dim] if dim in flips else own[dim] for dim in dims) + (EVERY, columns)
                last.append(sems.remote(buf.at[other], landing.at[mine], landing.at[other], across(*flips)))
                others.append(other)
            result.append((columns, mine, others))
        for wait in last:
            wait()
        return result

    for copy in wo_loads:
        copy.wait()
    for half in range(2):
        values[half] = jnp.dot(rel[half], vw_ref[...], preferred_element_type=F32).astype(BF)

    def project(half, target, columns):
        weight = jnp.concatenate([wo[q, :, columns] for q in range(4)], axis=1)
        product = jnp.dot(values[half], weight, preferred_element_type=F32).astype(BF)
        width = columns.size
        for q in range(4):
            block = product[:, q * width:(q + 1) * width].reshape(2, 2, 2, 16, width)
            target[:, :, :, q // 2, q % 2, :, columns] = block

    summed = reduce_scatter(project, sb, rbc, ab, rb, B_DIMS, B_GROUPS, B_PIECES)

    for wait in arrivals:
        wait()
    for j in range(4):
        hid[4 * j:4 * j + 4, :] = resx[j // 2, j % 2]
    block = tuple(own[dim] for dim in C_DIMS)
    squares = jnp.zeros((16, 1), F32)
    for columns, mine, others in summed:
        total = ab[mine].astype(F32)
        for other in others:
            total = total + rb[other].astype(F32)
        rounded = (hid[:, columns] + total).astype(BF)
        g[(core,) + block + (EVERY, columns)] = rounded
        total = rounded.astype(F32)
        hid[:, columns] = total
        squares = squares + jnp.sum(total * total, axis=1, keepdims=True)

    direct_waits = []
    for at, (_, direct) in enumerate(C_GROUPS):
        columns = pl.ds(at * HALF, HALF)
        here = g.at[(core,) + block + (EVERY, columns)]
        waits = []
        for flips in subsets(direct):
            other = tuple(1 - own[dim] if dim in flips else own[dim] for dim in C_DIMS)
            waits.append(sems.remote(here, here, g.at[(core,) + other + (EVERY, columns)], across(*flips)))
        direct_waits.append(waits)

    ss[0] = jnp.broadcast_to(squares, (16, 128))
    square_waits = [
        sems.remote(ss.at[0], ssr.at[x1, x0], ssr.at[p1, p0], device) for device, p1, p0 in lines
    ]
    for wait in square_waits:
        wait()
    squares = ss[0]
    for _, p1, p0 in lines:
        squares = squares + ssr[p1, p0]
    weights = jnp.concatenate([wx[j // 2, j % 2] for j in range(4)], axis=0)
    lanes = lax.broadcasted_iota(jnp.int32, (16, 128), 1)
    scale = lax.rsqrt(squares * (1.0 / D) + 1e-06)
    table_at = (core, own["z1"], own["z0"], own["y1"], own["y0"])
    tab[table_at] = jnp.where(lanes == EXPERTS, scale, weights)

    def table_step(first, second, others):
        dims = ("z1", "z0", "y1", "y0")

        def at(flips):
            indices = []
            for dim in dims:
                if dim in (first, second):
                    indices.append(1 - own[dim] if dim in flips else own[dim])
                else:
                    indices.append(EVERY if others else own[dim])
            return (core,) + tuple(indices)

        return [
            sems.remote(tab.at[at(())], tab.at[at(())], tab.at[at(flips)], across(*flips))
            for flips in subsets((first, second))
        ]

    found = all_pieces(C_GROUPS, C_PIECES)
    waits, forwards = [None] * len(found), []

    def gather_place(n, step, mine):
        at, columns, order = found[n]
        indices = []
        for dim in C_DIMS:
            if dim not in order or order.index(dim) < step:
                indices.append(EVERY)
            elif order.index(dim) == step:
                indices.append(own[dim] if mine else 1 - own[dim])
            else:
                indices.append(own[dim])
        return tuple(indices) + (EVERY, columns)

    def forward(n, mine):
        where = gather_place(n, 2, mine)
        here = g.at[(core,) + where]
        forwards.append(sems.remote(here, here, g.at[(sibling,) + where], twin))

    table_waits = table_step("y0", "z0", False)
    for step in range(4):
        for n in range(len(found)):
            if step:
                waits[n]()
            elif n < 2:
                for wait in direct_waits[n]:
                    wait()
            if step < 3:
                here = g.at[(core,) + gather_place(n, step, True)]
                there = g.at[(core,) + gather_place(n, step, False)]
                waits[n] = sems.remote(here, here, there, across(found[n][2][step]))
            if step > 1:
                forward(n, step == 2)
        if step < 3:
            for wait in table_waits:
                wait()
        if step == 0:
            table_waits = table_step("y1", "z1", True)
        elif step == 1:
            table_waits = [sems.remote(tab.at[core], tab.at[core], tab.at[sibling], twin)]

    wg_load.wait()
    wu_load.wait()
    expert = role * 8 + zl * 4 + y
    rows_lanes = lax.broadcasted_iota(jnp.int32, (256, 128), 1)

    def gate_up(half):
        accg[...] = jnp.zeros_like(accg)
        accu[...] = jnp.zeros_like(accu)

        def quarter(q, carry):
            rows = g[half, :, :, :, :, q // 2, q % 2].reshape(256, Q)
            accg[...] += jnp.dot(rows, wg[q], preferred_element_type=F32)
            accu[...] += jnp.dot(rows, wu[q], preferred_element_type=F32)
            return carry

        lax.fori_loop(0, 4, quarter, 0)

    def activate(half):
        table = tab[half].reshape(256, 128)
        weight = jnp.sum(jnp.where(rows_lanes == expert, table, 0.0), axis=1, keepdims=True)
        scale = jnp.sum(jnp.where(rows_lanes == EXPERTS, table, 0.0), axis=1, keepdims=True)
        gate = accg[...] * scale
        act[half] = (jax.nn.silu(gate) * (accu[...] * scale) * weight).astype(BF)

    gate_up(core)
    activate(core)
    for wait in forwards:
        wait()
    gate_up(sibling)
    activate(sibling)
    for copy in wd_loads:
        copy.wait()

    def down(half, target, columns):
        weight = jnp.concatenate([wd[q, :, columns] for q in range(4)], axis=1)
        product = jnp.dot(act[half], weight, preferred_element_type=F32).astype(BF)
        width = columns.size
        for q in range(4):
            block = product[:, q * width:(q + 1) * width].reshape(2, 2, 2, 2, 16, width)
            target[:, :, :, :, q // 2, q % 2, :, columns] = block

    summed = reduce_scatter(down, sh, rhc, ah, rh, C_DIMS, C_GROUPS, C_PIECES)
    for columns, mine, others in summed:
        total = hid[:, columns] + ah[mine].astype(F32)
        for other in others:
            total = total + rh[other].astype(F32)
        outs[:, columns] = total

    for j in range(4):
        fsend[j // 2, j % 2] = outs[4 * j:4 * j + 4, :]
    waits = [
        sems.remote(fsend.at[p1, p0], frecv.at[x1, x0], frecv.at[p1, p0], device)
        for device, p1, p0 in lines
    ]
    frecv[x1, x0] = fsend[x1, x0]
    for wait in waits:
        wait()
    for j in range(4):
        out_ref[:, j * Q:(j + 1) * Q] = frecv[j // 2, j % 2].astype(BF)
    assert sems.count <= SEMS
    everyone.wait_send()
    for copy in sems.pending:
        copy.wait_send()


def layer(*operands):
    vmem = pl.BlockSpec(memory_space=pltpu.VMEM)
    hbm = pl.BlockSpec(memory_space=pl.ANY)
    b_shape, c_shape = (2,) * 5 + (16, Q), (2,) * 6 + (16, Q)
    return pl.pallas_call(
        kernel,
        out_shape=jax.ShapeDtypeStruct((4, D), BF),
        in_specs=[pl.BlockSpec(memory_space=pltpu.SMEM)] + [vmem] * 4 + [hbm] * 6,
        out_specs=vmem,
        scratch_shapes=[
            pltpu.VMEM((4, HEADS, LATENT), BF),
            pltpu.VMEM((4, LATENT, LEN), BF),
            pltpu.VMEM((4, HEADS, KEY_VALUE_RANK), BF),
            pltpu.VMEM((HEADS, 16, 128), BF),
            pltpu.VMEM((HEADS, 16, 128), BF),
            pltpu.VMEM((2, 128, KEY_VALUE_RANK), BF),
            pltpu.VMEM((2, 2, 4, Q), F32),
            pltpu.VMEM((4, 128), F32),
            pltpu.SemaphoreType.DMA((2,)),
            pltpu.VMEM((4, HEAD, Q), BF),
            pltpu.VMEM((4, Q, FF), BF),
            pltpu.VMEM((4, Q, FF), BF),
            pltpu.VMEM((4, FF, Q), BF),
            pltpu.VMEM((2, 2, 4, Q), F32),
            pltpu.VMEM((2, 2, 4, 128), F32),
            pltpu.VMEM((16, Q), F32),
            pltpu.VMEM((2, 128, HEAD), BF),
            pltpu.VMEM(b_shape, BF),
            pltpu.VMEM(b_shape, BF),
            pltpu.VMEM(b_shape, BF),
            pltpu.VMEM(b_shape, BF),
            pltpu.VMEM((1, 16, 128), F32),
            pltpu.VMEM((2, 2, 16, 128), F32),
            pltpu.VMEM((2,) * 5 + (16, 128), F32),
            pltpu.VMEM((2,) + c_shape, BF),
            pltpu.VMEM((256, FF), F32),
            pltpu.VMEM((256, FF), F32),
            pltpu.VMEM((2, 256, FF), BF),
            pltpu.VMEM(c_shape, BF),
            pltpu.VMEM(c_shape, BF),
            pltpu.VMEM(c_shape, BF),
            pltpu.VMEM(c_shape, BF),
            pltpu.VMEM((16, Q), F32),
            pltpu.VMEM((2, 2, 4, Q), F32),
            pltpu.VMEM((2, 2, 4, Q), F32),
            pltpu.SemaphoreType.DMA((18,)),
            pltpu.SemaphoreType.DMA((SEMS,)),
            pltpu.SemaphoreType.DMA((SEMS,)),
        ],
        compiler_params=pltpu.CompilerParams(
            collective_id=0, has_side_effects=True, vmem_limit_bytes=58 * 2**20
        ),
    )(*operands)


def local(
    queries, latent_cache, cache_lengths, residual, expert_ids, route_weights,
    value_weight, w_out, w_gate, w_up, w_down,
):
    return layer(
        cache_lengths, residual, expert_ids, route_weights, value_weight[0], queries, latent_cache.transpose(0, 2, 1), w_out,
        w_gate.reshape(4, Q, FF), w_up.reshape(4, Q, FF), w_down[0],
    )


def solution(mesh):
    return jax.shard_map(
        local,
        mesh=mesh,
        in_specs=(
            P(("role", "dev"), None, None),
            P(("role", "dev"), None, None),
            P(("role", "dev")),
            P(("role", "dev"), None),
            P(("role", "dev"), None),
            P(("role", "dev"), None),
            P("dev", None, None),
            P("dev", None),
            P(("role", "dev"), None, None),
            P(("role", "dev"), None, None),
            P(("role", "dev"), None, None),
        ),
        out_specs=P(("role", "dev"), None),
        check_vma=False,
    )
```

time: 127 us -> 106 us (0.83)
  Pallas kernels: 121 us -> 104 us
  local copies, waits for them, and re-layouts: 5.79 us -> 1.46 us
    pallas_call x1, Pallas kernels: 121 us -> 104 us  [layer(): pl.pallas_call(kernel, out_shape=jax.ShapeDtypeStruct((4, D), BF), in_spe...]
    unnamed x2 -> x1, local copies, waits for them, and re-layouts: 5.79 us -> 1.46 us
where the time goes in v3:
time: 106 us; the launch traced here: 105 us
  Pallas kernels  104 us (98%)
  local copies, waits for them, and re-layouts  1.46 us (1%)
    pallas_call x1, Pallas kernels, layer(): pl.pallas_call(kernel, out_shape=jax.ShapeDtypeStruct((4, D), BF), in_spe...  104 us

profile of v3, /device:TPU:0, one launch (start us, length us, event | category | flops | bytes accessed | tf_op | source)
XLA Modules:
  0.0 105.4 jit_solution(166347403324274250)
XLA Ops:
  0.0 103.9 %shard_map.109 = bf16[4,7168]{1,0:T(4,128)(2,1)} custom-call(s32[4]{0:T(128)} %len_ref.1, bf16[4,7168]{1,0:T(4,128)(2,1)} %res_ref.1, s32[4,8]{1,0:T(4,128)} %ids_ref.1, f32[4,8]{1,0:T(4,128)} %rw_ref.1, bf16[512,128]{1,0:T(8,128)(2,1)} %bitcast.9, bf16[4,64,576]{2,1,0:T(8,128)(2,1)} %q_hbm.1, bf16[4,576,512]{2,1,0:T(8,128)(2,1)} %bitcast.8, ...), custom_call_target="tpu_custom_call" | custom-call | tf_op jit(solution)/shard_map/pallas_call | solution.py:441
  103.9 1.5 %copy.13 = bf16[4,7168]{1,0:T(4,128)(2,1)} copy(bf16[4,7168]{1,0:T(4,128)(2,1)} %shard_map.109) | data formatting | bytes 114688

commit v4 on v3

--- a/solution.py
+++ b/solution.py
@@ -9,6 +9,7 @@
 
 KEY_VALUE_RANK = 512
 HEADS = 64
+CHIPS = HEADS // 2
 LEN = 512
 LATENT = 576
 EXPERTS = 16
@@ -75,13 +76,13 @@
         ).wait_recv
 
 
-SEMS = 200
+SEMS = 160
 
 
 def kernel(
-    len_ref, res_ref, ids_ref, rw_ref, vw_ref, q_hbm, cache_hbm, wo_hbm, wg_hbm, wu_hbm, wd_hbm, out_ref,
-    qv, cv, lat, mbuf, lbuf, rel, resq, wts, a2a, wo, wg, wu, wd, resx, wx, hid, values, sb, ab, rbc, rb, ss, ssr, tab, g, accg, accu, act,
-    sh, ah, rhc, rh, outs, fsend, frecv, loads, sends, recvs,
+    len_ref, res_ref, ids_ref, rw_ref, vw_hbm, q_hbm, cache_hbm, wo_hbm, wg_hbm, wu_hbm, wd_hbm, out_ref,
+    qv, cv, lat, mbuf, lbuf, rel, resq, wts, a2a, vw, wo, wg, wu, wd, resx, wx, hid, values, ab, rb, ss, ssr, tab, g,
+    accg, accu, act, ah, rh, outs, fsend, frecv, loads, sends, recvs,
 ):
     role, dev = lax.axis_index("role"), lax.axis_index("dev")
     core, x, y, zl = dev % 2, (dev // 2) % 4, (dev // 8) % 4, dev // 32
@@ -108,19 +109,21 @@
         return copy
 
     attention_loads = [(load(q_hbm.at[n], qv.at[n]), load(cache_hbm.at[n], cv.at[n])) for n in range(4)]
-    wo_loads = [load(wo_hbm.at[:, pl.ds(q * Q, Q)], wo.at[q]) for q in range(4)]
-    wg_load, wu_load = load(wg_hbm, wg), load(wu_hbm, wu)
-    wd_loads = [load(wd_hbm.at[:, pl.ds(q * Q, Q)], wd.at[q]) for q in range(4)]
+    vw_load = load(vw_hbm, vw.at[core])
+    quarters = [pl.ds(q * Q, Q) for q in range(4)]
+    wo_loads = [load(wo_hbm.at[:, quarters[q]], wo.at[q, core]) for q in range(4)]
+    wg_load, wu_load = load(wg_hbm, wg.at[core]), load(wu_hbm, wu.at[core])
+    wd_loads = [load(wd_hbm.at[:, quarters[q]], wd.at[q, core]) for q in range(4)]
 
     barrier = pltpu.get_barrier_semaphore()
 
     def greet(d, carry):
-        pl.semaphore_signal(barrier, inc=1, device_id=(role, (dev + d) % HEADS), device_id_type=MESH)
+        pl.semaphore_signal(barrier, inc=1, device_id=(role, (dev + 2 * d) % HEADS), device_id_type=MESH)
         return carry
 
-    lax.fori_loop(1, HEADS, greet, 0)
+    lax.fori_loop(1, CHIPS, greet, 0)
     beyond = [across(*flips) for flips in subsets(("x1", "y1", "z1")) if "z1" in flips]
-    for device in beyond:
+    for device in [twin] + beyond:
         pl.semaphore_signal(barrier, inc=1, device_id=device, device_id_type=MESH)
 
     for q in range(4):
@@ -151,29 +154,34 @@
         heads = slice(16 * group, 16 * group + 16)
         pieces = [lat[n, heads, 128 * c:128 * c + 128] for c in range(4) for n in range(4)]
         moved = jnp.dot(regroup, jnp.concatenate(pieces, axis=0), preferred_element_type=F32)
-        mbuf[heads] = moved.astype(BF).reshape(16, 16, 128)
-
-    pl.semaphore_wait(barrier, HEADS - 1 + len(beyond))
-    seat = (((core * 2 + own["z0"]) * 2 + own["y1"]) * 2 + own["y0"]) * 4 + own["x1"] * 2 + own["x0"]
-
-    def message(head):
+        mbuf[8 * group:8 * group + 8] = moved.astype(BF).reshape(8, 2, 16, 128)
+
+    pl.semaphore_wait(barrier, CHIPS + len(beyond))
+    seat = ((own["z0"] * 2 + own["y1"]) * 2 + own["y0"]) * 4 + own["x1"] * 2 + own["x0"]
+
+    def message(chip):
         return pltpu.make_async_remote_copy(
-            src_ref=mbuf.at[head], dst_ref=lbuf.at[seat], send_sem=a2a.at[0], recv_sem=a2a.at[1],
-            device_id=(role, head), device_id_type=MESH,
+            src_ref=mbuf.at[chip], dst_ref=lbuf.at[seat], send_sem=a2a.at[0], recv_sem=a2a.at[1],
+            device_id=(role, 2 * chip + core), device_id_type=MESH,
         )
 
     def post(d, carry):
-        message((dev + d) % HEADS).start()
+        message((dev // 2 + d) % CHIPS).start()
         return carry
 
-    lax.fori_loop(1, HEADS, post, 0)
-    lbuf[seat] = mbuf[dev]
+    lax.fori_loop(1, CHIPS, post, 0)
+    lbuf[seat] = mbuf[dev // 2]
 
     sems = Sems(sends, recvs)
     x1, x0 = own["x1"], own["x0"]
     lines = (
         (across("x1", "x0"), 1 - x1, 1 - x0), (across("x1"), 1 - x1, x0), (across("x0"), x1, 1 - x0),
     )
+
+    vw_wait = sems.remote(vw_hbm, vw.at[core], vw.at[sibling], twin)
+    wo_waits = [
+        sems.remote(wo_hbm.at[:, quarters[q]], wo.at[q, core], wo.at[q, sibling], twin) for q in range(4)
+    ]
 
     arrivals = []
     for device, p1, p0 in lines:
@@ -181,21 +189,26 @@
         arrivals.append(sems.remote(wts, wx.at[x1, x0], wx.at[p1, p0], device))
     resx[x1, x0] = resq[x1, x0]
     wx[x1, x0] = wts[...]
+    wg_wait = sems.remote(wg_hbm, wg.at[core], wg.at[sibling], twin)
+    wu_wait = sems.remote(wu_hbm, wu.at[core], wu.at[sibling], twin)
+    wd_waits = [
+        sems.remote(wd_hbm.at[:, quarters[q]], wd.at[q, core], wd.at[q, sibling], twin) for q in range(4)
+    ]
 
     spread = jnp.where(source == ((to % 64) // 4) * 16 + (to // 64) * 4 + to % 4, 1.0, 0.0).astype(BF)
     everyone = pltpu.make_async_remote_copy(
-        src_ref=mbuf.at[pl.ds(0, HEADS - 1)], dst_ref=lbuf.at[pl.ds(0, HEADS - 1)],
+        src_ref=mbuf.at[pl.ds(0, CHIPS - 1)], dst_ref=lbuf.at[pl.ds(0, CHIPS - 1)],
         send_sem=a2a.at[0], recv_sem=a2a.at[1], device_id=twin, device_id_type=MESH,
     )
     everyone.wait_recv()
-    for group in range(4):
-        rows = lbuf[16 * group:16 * group + 16].reshape(256, 128)
-        moved = jnp.dot(spread, rows, preferred_element_type=F32).astype(BF)
-        for c in range(4):
-            rel[group // 2, 64 * (group % 2):64 * (group % 2) + 64, 128 * c:128 * c + 128] = moved[64 * c:64 * c + 64]
-
-    def reduce_scatter(produce, given, taken, buf, landing, dims, groups, pieces):
-        whole = (EVERY,) * (len(dims) + 1)
+    for group in range(2):
+        for head in range(2):
+            rows = lbuf[16 * group:16 * group + 16, head].reshape(256, 128)
+            moved = jnp.dot(spread, rows, preferred_element_type=F32).astype(BF)
+            for c in range(4):
+                rel[head, 64 * group:64 * group + 64, 128 * c:128 * c + 128] = moved[64 * c:64 * c + 64]
+
+    def reduce_scatter(produce, buf, landing, dims, groups, pieces):
         found = all_pieces(groups, pieces)
         waits = [None] * len(found)
 
@@ -216,22 +229,12 @@
         def add(n, step):
             _, columns, order = found[n]
             waits[n]()
-            if step < 0:
-                buf[whole + (columns,)] = buf[whole + (columns,)] + taken[whole + (columns,)]
-            else:
-                mine, other = place(order, step, True) + (columns,), place(order, step, False) + (columns,)
-                buf[mine] = buf[mine] + landing[other]
+            mine, other = place(order, step, True) + (columns,), place(order, step, False) + (columns,)
+            buf[mine] = buf[mine] + landing[other]
 
         for n, (_, columns, _) in enumerate(found):
-            produce(sibling, given, columns)
-            where = whole + (columns,)
-            waits[n] = sems.remote(given.at[where], taken.at[where], taken.at[where], twin)
-            produce(core, buf, columns)
-            if n:
-                add(n - 1, -1)
-                advance(n - 1, 0)
-        add(len(found) - 1, -1)
-        advance(len(found) - 1, 0)
+            produce(buf, columns)
+            advance(n, 0)
         rounds = len(groups[0][0])
         for step in range(1, rounds):
             for n in range(len(found)):
@@ -254,20 +257,26 @@
             wait()
         return result
 
+    vw_load.wait()
+    vw_wait()
+    for head in range(2):
+        values[:, HEAD * head:HEAD * head + HEAD] = jnp.dot(
+            rel[head], vw[head], preferred_element_type=F32
+        ).astype(BF)
     for copy in wo_loads:
         copy.wait()
-    for half in range(2):
-        values[half] = jnp.dot(rel[half], vw_ref[...], preferred_element_type=F32).astype(BF)
-
-    def project(half, target, columns):
-        weight = jnp.concatenate([wo[q, :, columns] for q in range(4)], axis=1)
-        product = jnp.dot(values[half], weight, preferred_element_type=F32).astype(BF)
+    for wait in wo_waits:
+        wait()
+
+    def project(target, columns):
         width = columns.size
+        weight = jnp.concatenate([wo[q, :, :, columns].reshape(2 * HEAD, width) for q in range(4)], axis=1)
+        product = jnp.dot(values[...], weight, preferred_element_type=F32).astype(BF)
         for q in range(4):
             block = product[:, q * width:(q + 1) * width].reshape(2, 2, 2, 16, width)
             target[:, :, :, q // 2, q % 2, :, columns] = block
 
-    summed = reduce_scatter(project, sb, rbc, ab, rb, B_DIMS, B_GROUPS, B_PIECES)
+    summed = reduce_scatter(project, ab, rb, B_DIMS, B_GROUPS, B_PIECES)
 
     for wait in arrivals:
         wait()
@@ -280,7 +289,7 @@
         for other in others:
             total = total + rb[other].astype(F32)
         rounded = (hid[:, columns] + total).astype(BF)
-        g[(core,) + block + (EVERY, columns)] = rounded
+        g[block + (EVERY, columns)] = rounded
         total = rounded.astype(F32)
         hid[:, columns] = total
         squares = squares + jnp.sum(total * total, axis=1, keepdims=True)
@@ -288,11 +297,11 @@
     direct_waits = []
     for at, (_, direct) in enumerate(C_GROUPS):
         columns = pl.ds(at * HALF, HALF)
-        here = g.at[(core,) + block + (EVERY, columns)]
+        here = g.at[block + (EVERY, columns)]
         waits = []
         for flips in subsets(direct):
             other = tuple(1 - own[dim] if dim in flips else own[dim] for dim in C_DIMS)
-            waits.append(sems.remote(here, here, g.at[(core,) + other + (EVERY, columns)], across(*flips)))
+            waits.append(sems.remote(here, here, g.at[other + (EVERY, columns)], across(*flips)))
         direct_waits.append(waits)
 
     ss[0] = jnp.broadcast_to(squares, (16, 128))
@@ -307,7 +316,7 @@
     weights = jnp.concatenate([wx[j // 2, j % 2] for j in range(4)], axis=0)
     lanes = lax.broadcasted_iota(jnp.int32, (16, 128), 1)
     scale = lax.rsqrt(squares * (1.0 / D) + 1e-06)
-    table_at = (core, own["z1"], own["z0"], own["y1"], own["y0"])
+    table_at = (own["z1"], own["z0"], own["y1"], own["y0"])
     tab[table_at] = jnp.where(lanes == EXPERTS, scale, weights)
 
     def table_step(first, second, others):
@@ -320,7 +329,7 @@
                     indices.append(1 - own[dim] if dim in flips else own[dim])
                 else:
                     indices.append(EVERY if others else own[dim])
-            return (core,) + tuple(indices)
+            return tuple(indices)
 
         return [
             sems.remote(tab.at[at(())], tab.at[at(())], tab.at[at(flips)], across(*flips))
@@ -328,7 +337,7 @@
         ]
 
     found = all_pieces(C_GROUPS, C_PIECES)
-    waits, forwards = [None] * len(found), []
+    waits = [None] * len(found)
 
     def gather_place(n, step, mine):
         at, columns, order = found[n]
@@ -342,75 +351,61 @@
                 indices.append(own[dim])
         return tuple(indices) + (EVERY, columns)
 
-    def forward(n, mine):
-        where = gather_place(n, 2, mine)
-        here = g.at[(core,) + where]
-        forwards.append(sems.remote(here, here, g.at[(sibling,) + where], twin))
-
     table_waits = table_step("y0", "z0", False)
-    for step in range(4):
+    for step in range(3):
         for n in range(len(found)):
             if step:
                 waits[n]()
             elif n < 2:
                 for wait in direct_waits[n]:
                     wait()
-            if step < 3:
-                here = g.at[(core,) + gather_place(n, step, True)]
-                there = g.at[(core,) + gather_place(n, step, False)]
-                waits[n] = sems.remote(here, here, there, across(found[n][2][step]))
-            if step > 1:
-                forward(n, step == 2)
-        if step < 3:
+            here = g.at[gather_place(n, step, True)]
+            there = g.at[gather_place(n, step, False)]
+            waits[n] = sems.remote(here, here, there, across(found[n][2][step]))
+        if step < 2:
             for wait in table_waits:
                 wait()
         if step == 0:
             table_waits = table_step("y1", "z1", True)
-        elif step == 1:
-            table_waits = [sems.remote(tab.at[core], tab.at[core], tab.at[sibling], twin)]
 
     wg_load.wait()
     wu_load.wait()
+    wg_wait()
+    wu_wait()
+    for n, (_, columns, _) in enumerate(found):
+        waits[n]()
+        width = columns.size
+        rows = jnp.concatenate(
+            [g[:, :, :, :, q // 2, q % 2, :, columns].reshape(256, width) for q in range(4)], axis=1
+        )
+        for unit in range(2):
+            for acc, weights in ((accg, wg), (accu, wu)):
+                weight = jnp.concatenate([weights[unit, q, columns, :] for q in range(4)], axis=0)
+                product = jnp.dot(rows, weight, preferred_element_type=F32)
+                acc[unit] = acc[unit] + product if n else product
     expert = role * 8 + zl * 4 + y
     rows_lanes = lax.broadcasted_iota(jnp.int32, (256, 128), 1)
-
-    def gate_up(half):
-        accg[...] = jnp.zeros_like(accg)
-        accu[...] = jnp.zeros_like(accu)
-
-        def quarter(q, carry):
-            rows = g[half, :, :, :, :, q // 2, q % 2].reshape(256, Q)
-            accg[...] += jnp.dot(rows, wg[q], preferred_element_type=F32)
-            accu[...] += jnp.dot(rows, wu[q], preferred_element_type=F32)
-            return carry
-
-        lax.fori_loop(0, 4, quarter, 0)
-
-    def activate(half):
-        table = tab[half].reshape(256, 128)
-        weight = jnp.sum(jnp.where(rows_lanes == expert, table, 0.0), axis=1, keepdims=True)
-        scale = jnp.sum(jnp.where(rows_lanes == EXPERTS, table, 0.0), axis=1, keepdims=True)
-        gate = accg[...] * scale
-        act[half] = (jax.nn.silu(gate) * (accu[...] * scale) * weight).astype(BF)
-
-    gate_up(core)
-    activate(core)
-    for wait in forwards:
-        wait()
-    gate_up(sibling)
-    activate(sibling)
+    table = tab[...].reshape(256, 128)
+    route = jnp.sum(jnp.where(rows_lanes == expert, table, 0.0), axis=1, keepdims=True)
+    scale = jnp.sum(jnp.where(rows_lanes == EXPERTS, table, 0.0), axis=1, keepdims=True)
+    for unit in range(2):
+        gate = accg[unit] * scale
+        activated = jax.nn.silu(gate) * (accu[unit] * scale) * route
+        act[:, FF * unit:FF * unit + FF] = activated.astype(BF)
     for copy in wd_loads:
         copy.wait()
-
-    def down(half, target, columns):
-        weight = jnp.concatenate([wd[q, :, columns] for q in range(4)], axis=1)
-        product = jnp.dot(act[half], weight, preferred_element_type=F32).astype(BF)
+    for wait in wd_waits:
+        wait()
+
+    def down(target, columns):
         width = columns.size
+        weight = jnp.concatenate([wd[q, :, :, columns].reshape(2 * FF, width) for q in range(4)], axis=1)
+        product = jnp.dot(act[...], weight, preferred_element_type=F32).astype(BF)
         for q in range(4):
             block = product[:, q * width:(q + 1) * width].reshape(2, 2, 2, 2, 16, width)
             target[:, :, :, :, q // 2, q % 2, :, columns] = block
 
-    summed = reduce_scatter(down, sh, rhc, ah, rh, C_DIMS, C_GROUPS, C_PIECES)
+    summed = reduce_scatter(down, ah, rh, C_DIMS, C_GROUPS, C_PIECES)
     for columns, mine, others in summed:
         total = hid[:, columns] + ah[mine].astype(F32)
         for other in others:
@@ -441,45 +436,42 @@
     return pl.pallas_call(
         kernel,
         out_shape=jax.ShapeDtypeStruct((4, D), BF),
-        in_specs=[pl.BlockSpec(memory_space=pltpu.SMEM)] + [vmem] * 4 + [hbm] * 6,
+        in_specs=[pl.BlockSpec(memory_space=pltpu.SMEM)] + [vmem] * 3 + [hbm] * 7,
         out_specs=vmem,
         scratch_shapes=[
             pltpu.VMEM((4, HEADS, LATENT), BF),
             pltpu.VMEM((4, LATENT, LEN), BF),
             pltpu.VMEM((4, HEADS, KEY_VALUE_RANK), BF),
-            pltpu.VMEM((HEADS, 16, 128), BF),
-            pltpu.VMEM((HEADS, 16, 128), BF),
+            pltpu.VMEM((CHIPS, 2, 16, 128), BF),
+            pltpu.VMEM((CHIPS, 2, 16, 128), BF),
             pltpu.VMEM((2, 128, KEY_VALUE_RANK), BF),
             pltpu.VMEM((2, 2, 4, Q), F32),
             pltpu.VMEM((4, 128), F32),
             pltpu.SemaphoreType.DMA((2,)),
-            pltpu.VMEM((4, HEAD, Q), BF),
-            pltpu.VMEM((4, Q, FF), BF),
-            pltpu.VMEM((4, Q, FF), BF),
-            pltpu.VMEM((4, FF, Q), BF),
+            pltpu.VMEM((2, KEY_VALUE_RANK, HEAD), BF),
+            pltpu.VMEM((4, 2, HEAD, Q), BF),
+            pltpu.VMEM((2, 4, Q, FF), BF),
+            pltpu.VMEM((2, 4, Q, FF), BF),
+            pltpu.VMEM((4, 2, FF, Q), BF),
             pltpu.VMEM((2, 2, 4, Q), F32),
             pltpu.VMEM((2, 2, 4, 128), F32),
             pltpu.VMEM((16, Q), F32),
-            pltpu.VMEM((2, 128, HEAD), BF),
-            pltpu.VMEM(b_shape, BF),
-            pltpu.VMEM(b_shape, BF),
+            pltpu.VMEM((128, 2 * HEAD), BF),
             pltpu.VMEM(b_shape, BF),
             pltpu.VMEM(b_shape, BF),
             pltpu.VMEM((1, 16, 128), F32),
             pltpu.VMEM((2, 2, 16, 128), F32),
-            pltpu.VMEM((2,) * 5 + (16, 128), F32),
-            pltpu.VMEM((2,) + c_shape, BF),
-            pltpu.VMEM((256, FF), F32),
-            pltpu.VMEM((256, FF), F32),
-            pltpu.VMEM((2, 256, FF), BF),
+            pltpu.VMEM((2,) * 4 + (16, 128), F32),
             pltpu.VMEM(c_shape, BF),
-            pltpu.VMEM(c_shape, BF),
+            pltpu.VMEM((2, 256, FF), F32),
+            pltpu.VMEM((2, 256, FF), F32),
+            pltpu.VMEM((256, 2 * FF), BF),
             pltpu.VMEM(c_shape, BF),
             pltpu.VMEM(c_shape, BF),
             pltpu.VMEM((16, Q), F32),
             pltpu.VMEM((2, 2, 4, Q), F32),
             pltpu.VMEM((2, 2, 4, Q), F32),
-            pltpu.SemaphoreType.DMA((18,)),
+            pltpu.SemaphoreType.DMA((19,)),
             pltpu.SemaphoreType.DMA((SEMS,)),
             pltpu.SemaphoreType.DMA((SEMS,)),
         ],

time: 106 us -> 91.9 us (0.87)
  Pallas kernels: 104 us -> 90.2 us
    pallas_call x1, Pallas kernels: 104 us -> 90.2 us  [layer(): pl.pallas_call(kernel, out_shape=jax.ShapeDtypeStruct((4, D), BF), in_spe...]
where the time goes in v4:
time: 91.9 us; the launch traced here: 91.7 us
  Pallas kernels  90.2 us (98%)
  local copies, waits for them, and re-layouts  1.46 us (2%)
    pallas_call x1, Pallas kernels, layer(): pl.pallas_call(kernel, out_shape=jax.ShapeDtypeStruct((4, D), BF), in_spe...  90.2 us

profile of v4, /device:TPU:0, one launch (start us, length us, event | category | flops | bytes accessed | tf_op | source)
XLA Modules:
  0.0 91.7 jit_solution(15819023307895557180)
XLA Ops:
  0.0 90.2 %shard_map.109 = bf16[4,7168]{1,0:T(4,128)(2,1)} custom-call(s32[4]{0:T(128)} %len_ref.1, bf16[4,7168]{1,0:T(4,128)(2,1)} %res_ref.1, s32[4,8]{1,0:T(4,128)} %ids_ref.1, f32[4,8]{1,0:T(4,128)} %rw_ref.1, bf16[512,128]{1,0:T(8,128)(2,1)} %bitcast.9, bf16[4,64,576]{2,1,0:T(8,128)(2,1)} %q_hbm.1, bf16[4,576,512]{2,1,0:T(8,128)(2,1)} %bitcast.8, ...), custom_call_target="tpu_custom_call" | custom-call | tf_op jit(solution)/shard_map/pallas_call | solution.py:436
  90.2 1.5 %copy.13 = bf16[4,7168]{1,0:T(4,128)(2,1)} copy(bf16[4,7168]{1,0:T(4,128)(2,1)} %shard_map.109) | data formatting | bytes 114688

commit v5 on v4

--- a/solution.py
+++ b/solution.py
@@ -27,17 +27,22 @@
 C_DIMS = ("z1",) + B_DIMS
 HALF = Q // 2
 B_GROUPS = ((("x1", "y1"), ("x0", "y0", "z0")), (("x0", "y0"), ("x1", "y1", "z0")))
-B_PIECES = ((0, 2, 0), (4, 2, 1), (2, 2, 0), (6, 1, 1))
+B_PIECES = (
+    (0, 2, 0, None), (3, 2, 1, None), (2, 1, 0, None), (5, 1, 1, None), (6, 1, 0, 0), (6, 1, 1, 1),
+)
 C_GROUPS = ((("x1", "y1", "z1"), ("x0", "y0", "z0")), (("x0", "y0", "z0"), ("x1", "y1", "z1")))
-C_PIECES = ((0, 2, 0), (3, 1, 1), (5, 1, 2), (2, 1, 0), (4, 1, 1), (6, 1, 2))
+C_PIECES = (
+    (0, 1, 0, None), (3, 1, 1, None), (5, 1, 2, None), (1, 1, 0, None), (4, 1, 1, None), (6, 1, 2, None),
+    (2, 1, 0, 0), (2, 1, 1, 1),
+)
 
 
 def all_pieces(groups, pieces):
     found = []
-    for tile, count, turn in pieces:
-        for at, (ring, _) in enumerate(groups):
+    for tile, count, turn, half in pieces:
+        for at, (ring, direct) in enumerate(groups):
             columns = pl.ds(at * HALF + tile * 128, count * 128)
-            found.append((at, columns, ring[turn:] + ring[:turn]))
+            found.append((at, columns, ring[turn:] + ring[:turn], {} if half is None else {direct[0]: half}))
     return found
 
 
@@ -76,7 +81,7 @@
         ).wait_recv
 
 
-SEMS = 160
+SEMS = 192
 
 
 def kernel(
@@ -212,28 +217,32 @@
         found = all_pieces(groups, pieces)
         waits = [None] * len(found)
 
-        def place(order, step, mine):
+        def place(n, step, mine):
+            _, columns, order, confined = found[n]
             indices = []
             for dim in dims:
+                if dim in confined:
+                    indices.append(confined[dim])
+                    continue
                 at = order.index(dim) if dim in order else len(order)
                 here = own[dim] if mine else 1 - own[dim]
                 indices.append(own[dim] if at < step else here if at == step else EVERY)
-            return tuple(indices) + (EVERY,)
+            return tuple(indices) + (EVERY, columns)
 
         def advance(n, step):
-            _, columns, order = found[n]
-            mine, other = place(order, step, True) + (columns,), place(order, step, False) + (columns,)
+            order = found[n][2]
+            mine, other = place(n, step, True), place(n, step, False)
             if step < len(order):
                 waits[n] = sems.remote(buf.at[other], landing.at[mine], landing.at[other], across(order[step]))
 
         def add(n, step):
-            _, columns, order = found[n]
             waits[n]()
-            mine, other = place(order, step, True) + (columns,), place(order, step, False) + (columns,)
+            mine, other = place(n, step, True), place(n, step, False)
             buf[mine] = buf[mine] + landing[other]
 
-        for n, (_, columns, _) in enumerate(found):
-            produce(buf, columns)
+        for n, (_, columns, _, confined) in enumerate(found):
+            if 1 not in confined.values():
+                produce(buf, columns)
             advance(n, 0)
         rounds = len(groups[0][0])
         for step in range(1, rounds):
@@ -340,10 +349,12 @@
     waits = [None] * len(found)
 
     def gather_place(n, step, mine):
-        at, columns, order = found[n]
+        _, columns, order, confined = found[n]
         indices = []
         for dim in C_DIMS:
-            if dim not in order or order.index(dim) < step:
+            if dim in confined:
+                indices.append(confined[dim])
+            elif dim not in order or order.index(dim) < step:
                 indices.append(EVERY)
             elif order.index(dim) == step:
                 indices.append(own[dim] if mine else 1 - own[dim])
@@ -372,17 +383,28 @@
     wu_load.wait()
     wg_wait()
     wu_wait()
-    for n, (_, columns, _) in enumerate(found):
+    batch, first = [], True
+    for n, (_, columns, _, confined) in enumerate(found):
         waits[n]()
-        width = columns.size
+        if 0 not in confined.values():
+            batch.append(columns)
+        if n % 6 < 5 and n < len(found) - 1:
+            continue
         rows = jnp.concatenate(
-            [g[:, :, :, :, q // 2, q % 2, :, columns].reshape(256, width) for q in range(4)], axis=1
+            [
+                g[:, :, :, :, q // 2, q % 2, :, tile].reshape(256, tile.size)
+                for tile in batch for q in range(4)
+            ],
+            axis=1,
         )
         for unit in range(2):
             for acc, weights in ((accg, wg), (accu, wu)):
-                weight = jnp.concatenate([weights[unit, q, columns, :] for q in range(4)], axis=0)
+                weight = jnp.concatenate(
+                    [weights[unit, q, tile, :] for tile in batch for q in range(4)], axis=0
+                )
                 product = jnp.dot(rows, weight, preferred_element_type=F32)
-                acc[unit] = acc[unit] + product if n else product
+                acc[unit] = product if first else acc[unit] + product
+        batch, first = [], False
     expert = role * 8 + zl * 4 + y
     rows_lanes = lax.broadcasted_iota(jnp.int32, (256, 128), 1)
     table = tab[...].reshape(256, 128)

time: 91.9 us -> 90.1 us (0.980)
  Pallas kernels: 90.2 us -> 88.5 us
    pallas_call x1, Pallas kernels: 90.2 us -> 88.5 us  [layer(): pl.pallas_call(kernel, out_shape=jax.ShapeDtypeStruct((4, D), BF), in_spe...]
where the time goes in v5:
time: 90.1 us; the launch traced here: 89.9 us
  Pallas kernels  88.5 us (98%)
  local copies, waits for them, and re-layouts  1.46 us (2%)
    pallas_call x1, Pallas kernels, layer(): pl.pallas_call(kernel, out_shape=jax.ShapeDtypeStruct((4, D), BF), in_spe...  88.5 us

profile of v5, /device:TPU:0, one launch (start us, length us, event | category | flops | bytes accessed | tf_op | source)
XLA Modules:
  0.0 89.9 jit_solution(3909445442402158594)
XLA Ops:
  0.0 88.5 %shard_map.109 = bf16[4,7168]{1,0:T(4,128)(2,1)} custom-call(s32[4]{0:T(128)} %len_ref.1, bf16[4,7168]{1,0:T(4,128)(2,1)} %res_ref.1, s32[4,8]{1,0:T(4,128)} %ids_ref.1, f32[4,8]{1,0:T(4,128)} %rw_ref.1, bf16[512,128]{1,0:T(8,128)(2,1)} %bitcast.9, bf16[4,64,576]{2,1,0:T(8,128)(2,1)} %q_hbm.1, bf16[4,576,512]{2,1,0:T(8,128)(2,1)} %bitcast.8, ...), custom_call_target="tpu_custom_call" | custom-call | tf_op jit(solution)/shard_map/pallas_call | solution.py:458
  88.5 1.5 %copy.13 = bf16[4,7168]{1,0:T(4,128)(2,1)} copy(bf16[4,7168]{1,0:T(4,128)(2,1)} %shard_map.109) | data formatting | bytes 114688

commit v6 on v5

--- a/solution.py
+++ b/solution.py
@@ -57,6 +57,11 @@
 class Sems:
     def __init__(self, sends, recvs):
         self.sends, self.recvs, self.count, self.pending = sends, recvs, 0, []
+
+    def drain(self, count):
+        for copy in self.pending[:count]:
+            copy.wait_send()
+        self.pending = self.pending[count:]
 
     def remote(self, source, target, landing, device):
         n = self.count
@@ -120,6 +125,7 @@
     wg_load, wu_load = load(wg_hbm, wg.at[core]), load(wu_hbm, wu.at[core])
     wd_loads = [load(wd_hbm.at[:, quarters[q]], wd.at[q, core]) for q in range(4)]
 
+    sems = Sems(sends, recvs)
     barrier = pltpu.get_barrier_semaphore()
 
     def greet(d, carry):
@@ -143,14 +149,25 @@
     for pair in attention_loads:
         for copy in pair:
             copy.wait()
-    scores = [jnp.dot(qv[n], cv[n], preferred_element_type=F32) * score_scale for n in range(4)]
-    for n in range(4):
-        live = jnp.where(slots < len_ref[n], scores[n], -jnp.inf)
-        raised = jnp.exp(live - jnp.max(live, axis=1, keepdims=True))
-        chances = (raised / jnp.sum(raised, axis=1, keepdims=True)).astype(BF)
-        lat[n] = lax.dot_general(
-            chances, cv[n, :KEY_VALUE_RANK, :], (((1,), (1,)), ((), ())), preferred_element_type=F32
-        ).astype(BF)
+    def attend(requests):
+        scores = [jnp.dot(qv[n], cv[n], preferred_element_type=F32) * score_scale for n in requests]
+        for n, score in zip(requests, scores):
+            live = jnp.where(slots < len_ref[n], score, -jnp.inf)
+            raised = jnp.exp(live - jnp.max(live, axis=1, keepdims=True))
+            chances = (raised / jnp.sum(raised, axis=1, keepdims=True)).astype(BF)
+            lat[n] = lax.dot_general(
+                chances, cv[n, :KEY_VALUE_RANK, :], (((1,), (1,)), ((), ())), preferred_element_type=F32
+            ).astype(BF)
+
+    attend((0, 1))
+
+    pl.semaphore_wait(barrier, CHIPS + len(beyond))
+    vw_wait = sems.remote(vw_hbm, vw.at[core], vw.at[sibling], twin)
+    wo_waits = [
+        sems.remote(wo_hbm.at[:, quarters[q]], wo.at[q, core], wo.at[q, sibling], twin) for q in range(4)
+    ]
+
+    attend((2, 3))
 
     to = lax.broadcasted_iota(jnp.int32, (256, 256), 0)
     source = lax.broadcasted_iota(jnp.int32, (256, 256), 1)
@@ -161,7 +178,6 @@
         moved = jnp.dot(regroup, jnp.concatenate(pieces, axis=0), preferred_element_type=F32)
         mbuf[8 * group:8 * group + 8] = moved.astype(BF).reshape(8, 2, 16, 128)
 
-    pl.semaphore_wait(barrier, CHIPS + len(beyond))
     seat = ((own["z0"] * 2 + own["y1"]) * 2 + own["y0"]) * 4 + own["x1"] * 2 + own["x0"]
 
     def message(chip):
@@ -177,16 +193,10 @@
     lax.fori_loop(1, CHIPS, post, 0)
     lbuf[seat] = mbuf[dev // 2]
 
-    sems = Sems(sends, recvs)
     x1, x0 = own["x1"], own["x0"]
     lines = (
         (across("x1", "x0"), 1 - x1, 1 - x0), (across("x1"), 1 - x1, x0), (across("x0"), x1, 1 - x0),
     )
-
-    vw_wait = sems.remote(vw_hbm, vw.at[core], vw.at[sibling], twin)
-    wo_waits = [
-        sems.remote(wo_hbm.at[:, quarters[q]], wo.at[q, core], wo.at[q, sibling], twin) for q in range(4)
-    ]
 
     arrivals = []
     for device, p1, p0 in lines:
@@ -194,11 +204,14 @@
         arrivals.append(sems.remote(wts, wx.at[x1, x0], wx.at[p1, p0], device))
     resx[x1, x0] = resq[x1, x0]
     wx[x1, x0] = wts[...]
+    early = len(sems.pending)
     wg_wait = sems.remote(wg_hbm, wg.at[core], wg.at[sibling], twin)
     wu_wait = sems.remote(wu_hbm, wu.at[core], wu.at[sibling], twin)
     wd_waits = [
         sems.remote(wd_hbm.at[:, quarters[q]], wd.at[q, core], wd.at[q, sibling], twin) for q in range(4)
     ]
+
+    late, sems.pending = sems.pending[early:], sems.pending[:early]
 
     spread = jnp.where(source == ((to % 64) // 4) * 16 + (to // 64) * 4 + to % 4, 1.0, 0.0).astype(BF)
     everyone = pltpu.make_async_remote_copy(
@@ -215,7 +228,7 @@
 
     def reduce_scatter(produce, buf, landing, dims, groups, pieces):
         found = all_pieces(groups, pieces)
-        waits = [None] * len(found)
+        waits, before = [None] * len(found), len(sems.pending)
 
         def place(n, step, mine):
             _, columns, order, confined = found[n]
@@ -244,12 +257,14 @@
             if 1 not in confined.values():
                 produce(buf, columns)
             advance(n, 0)
+        sems.drain(before)
         rounds = len(groups[0][0])
         for step in range(1, rounds):
             for n in range(len(found)):
                 add(n, step - 1)
                 advance(n, step)
         result, last = [], []
+        before = len(sems.pending)
         for at, (ring, direct) in enumerate(groups):
             columns = pl.ds(at * HALF, HALF)
             for n in range(len(found)):
@@ -262,6 +277,7 @@
                 last.append(sems.remote(buf.at[other], landing.at[mine], landing.at[other], across(*flips)))
                 others.append(other)
             result.append((columns, mine, others))
+        sems.drain(before)
         for wait in last:
             wait()
         return result
@@ -303,7 +319,7 @@
         hid[:, columns] = total
         squares = squares + jnp.sum(total * total, axis=1, keepdims=True)
 
-    direct_waits = []
+    direct_waits, before = [], len(sems.pending)
     for at, (_, direct) in enumerate(C_GROUPS):
         columns = pl.ds(at * HALF, HALF)
         here = g.at[block + (EVERY, columns)]
@@ -317,6 +333,7 @@
     square_waits = [
         sems.remote(ss.at[0], ssr.at[x1, x0], ssr.at[p1, p0], device) for device, p1, p0 in lines
     ]
+    sems.drain(before)
     for wait in square_waits:
         wait()
     squares = ss[0]
@@ -364,6 +381,7 @@
 
     table_waits = table_step("y0", "z0", False)
     for step in range(3):
+        before = len(sems.pending)
         for n in range(len(found)):
             if step:
                 waits[n]()
@@ -373,6 +391,8 @@
             here = g.at[gather_place(n, step, True)]
             there = g.at[gather_place(n, step, False)]
             waits[n] = sems.remote(here, here, there, across(found[n][2][step]))
+        if step:
+            sems.drain(before)
         if step < 2:
             for wait in table_waits:
                 wait()
@@ -383,6 +403,17 @@
     wu_load.wait()
     wg_wait()
     wu_wait()
+    for copy in wd_loads:
+        copy.wait()
+    for wait in wd_waits:
+        wait()
+    for copy in late:
+        copy.wait_send()
+    expert = role * 8 + zl * 4 + y
+    rows_lanes = lax.broadcasted_iota(jnp.int32, (256, 128), 1)
+    table = tab[...].reshape(256, 128)
+    route = jnp.sum(jnp.where(rows_lanes == expert, table, 0.0), axis=1, keepdims=True)
+    scale = jnp.sum(jnp.where(rows_lanes == EXPERTS, table, 0.0), axis=1, keepdims=True)
     batch, first = [], True
     for n, (_, columns, _, confined) in enumerate(found):
         waits[n]()
@@ -405,19 +436,10 @@
                 product = jnp.dot(rows, weight, preferred_element_type=F32)
                 acc[unit] = product if first else acc[unit] + product
         batch, first = [], False
-    expert = role * 8 + zl * 4 + y
-    rows_lanes = lax.broadcasted_iota(jnp.int32, (256, 128), 1)
-    table = tab[...].reshape(256, 128)
-    route = jnp.sum(jnp.where(rows_lanes == expert, table, 0.0), axis=1, keepdims=True)
-    scale = jnp.sum(jnp.where(rows_lanes == EXPERTS, table, 0.0), axis=1, keepdims=True)
     for unit in range(2):
         gate = accg[unit] * scale
         activated = jax.nn.silu(gate) * (accu[unit] * scale) * route
         act[:, FF * unit:FF * unit + FF] = activated.astype(BF)
-    for copy in wd_loads:
-        copy.wait()
-    for wait in wd_waits:
-        wait()
 
     def down(target, columns):
         width = columns.size
@@ -436,19 +458,20 @@
 
     for j in range(4):
         fsend[j // 2, j % 2] = outs[4 * j:4 * j + 4, :]
+    before = len(sems.pending)
     waits = [
         sems.remote(fsend.at[p1, p0], frecv.at[x1, x0], frecv.at[p1, p0], device)
         for device, p1, p0 in lines
     ]
     frecv[x1, x0] = fsend[x1, x0]
+    everyone.wait_send()
+    sems.drain(before)
     for wait in waits:
         wait()
     for j in range(4):
         out_ref[:, j * Q:(j + 1) * Q] = frecv[j // 2, j % 2].astype(BF)
     assert sems.count <= SEMS
-    everyone.wait_send()
-    for copy in sems.pending:
-        copy.wait_send()
+    sems.drain(len(sems.pending))
 
 
 def layer(*operands):

time: 90.1 us -> 90.9 us (level)
  no operation moved by 1% of the time
where the time goes in v6:
time: 90.9 us; the launch traced here: 90.7 us
  Pallas kernels  89.2 us (98%)
  local copies, waits for them, and re-layouts  1.46 us (2%)
    pallas_call x1, Pallas kernels, layer(): pl.pallas_call(kernel, out_shape=jax.ShapeDtypeStruct((4, D), BF), in_spe...  89.2 us

profile of v6, /device:TPU:0, one launch (start us, length us, event | category | flops | bytes accessed | tf_op | source)
XLA Modules:
  0.0 90.7 jit_solution(8697394156554177195)
XLA Ops:
  0.0 89.2 %shard_map.109 = bf16[4,7168]{1,0:T(4,128)(2,1)} custom-call(s32[4]{0:T(128)} %len_ref.1, bf16[4,7168]{1,0:T(4,128)(2,1)} %res_ref.1, s32[4,8]{1,0:T(4,128)} %ids_ref.1, f32[4,8]{1,0:T(4,128)} %rw_ref.1, bf16[512,128]{1,0:T(8,128)(2,1)} %bitcast.9, bf16[4,64,576]{2,1,0:T(8,128)(2,1)} %q_hbm.1, bf16[4,576,512]{2,1,0:T(8,128)(2,1)} %bitcast.8, ...), custom_call_target="tpu_custom_call" | custom-call | tf_op jit(solution)/shard_map/pallas_call | solution.py:481
  89.3 1.5 %copy.13 = bf16[4,7168]{1,0:T(4,128)(2,1)} copy(bf16[4,7168]{1,0:T(4,128)(2,1)} %shard_map.109) | data formatting | bytes 114688

commit v7 on v6

--- a/solution.py
+++ b/solution.py
@@ -86,7 +86,7 @@
         ).wait_recv
 
 
-SEMS = 192
+SEMS = 196
 
 
 def kernel(
@@ -159,15 +159,7 @@
                 chances, cv[n, :KEY_VALUE_RANK, :], (((1,), (1,)), ((), ())), preferred_element_type=F32
             ).astype(BF)
 
-    attend((0, 1))
-
-    pl.semaphore_wait(barrier, CHIPS + len(beyond))
-    vw_wait = sems.remote(vw_hbm, vw.at[core], vw.at[sibling], twin)
-    wo_waits = [
-        sems.remote(wo_hbm.at[:, quarters[q]], wo.at[q, core], wo.at[q, sibling], twin) for q in range(4)
-    ]
-
-    attend((2, 3))
+    attend((0, 1, 2, 3))
 
     to = lax.broadcasted_iota(jnp.int32, (256, 256), 0)
     source = lax.broadcasted_iota(jnp.int32, (256, 256), 1)
@@ -178,6 +170,7 @@
         moved = jnp.dot(regroup, jnp.concatenate(pieces, axis=0), preferred_element_type=F32)
         mbuf[8 * group:8 * group + 8] = moved.astype(BF).reshape(8, 2, 16, 128)
 
+    pl.semaphore_wait(barrier, CHIPS + len(beyond))
     seat = ((own["z0"] * 2 + own["y1"]) * 2 + own["y0"]) * 4 + own["x1"] * 2 + own["x0"]
 
     def message(chip):
@@ -197,6 +190,11 @@
     lines = (
         (across("x1", "x0"), 1 - x1, 1 - x0), (across("x1"), 1 - x1, x0), (across("x0"), x1, 1 - x0),
     )
+
+    vw_wait = sems.remote(vw_hbm, vw.at[core], vw.at[sibling], twin)
+    wo_waits = [
+        sems.remote(wo_hbm.at[:, quarters[q]], wo.at[q, core], wo.at[q, sibling], twin) for q in range(4)
+    ]
 
     arrivals = []
     for device, p1, p0 in lines:
@@ -263,7 +261,7 @@
             for n in range(len(found)):
                 add(n, step - 1)
                 advance(n, step)
-        result, last = [], []
+        result = []
         before = len(sems.pending)
         for at, (ring, direct) in enumerate(groups):
             columns = pl.ds(at * HALF, HALF)
@@ -271,15 +269,13 @@
                 if found[n][0] == at:
                     add(n, rounds - 1)
             mine = tuple(own[dim] for dim in dims) + (EVERY, columns)
-            others = []
+            others, last = [], []
             for flips in subsets(direct):
                 other = tuple(1 - own[dim] if dim in flips else own[dim] for dim in dims) + (EVERY, columns)
                 last.append(sems.remote(buf.at[other], landing.at[mine], landing.at[other], across(*flips)))
                 others.append(other)
-            result.append((columns, mine, others))
+            result.append((columns, mine, others, last))
         sems.drain(before)
-        for wait in last:
-            wait()
         return result
 
     vw_load.wait()
@@ -309,25 +305,24 @@
         hid[4 * j:4 * j + 4, :] = resx[j // 2, j % 2]
     block = tuple(own[dim] for dim in C_DIMS)
     squares = jnp.zeros((16, 1), F32)
-    for columns, mine, others in summed:
+    direct_waits, before = [], len(sems.pending)
+    for (columns, mine, others, last), (_, direct) in zip(summed, C_GROUPS):
+        for wait in last:
+            wait()
         total = ab[mine].astype(F32)
         for other in others:
             total = total + rb[other].astype(F32)
         rounded = (hid[:, columns] + total).astype(BF)
         g[block + (EVERY, columns)] = rounded
-        total = rounded.astype(F32)
-        hid[:, columns] = total
-        squares = squares + jnp.sum(total * total, axis=1, keepdims=True)
-
-    direct_waits, before = [], len(sems.pending)
-    for at, (_, direct) in enumerate(C_GROUPS):
-        columns = pl.ds(at * HALF, HALF)
         here = g.at[block + (EVERY, columns)]
         waits = []
         for flips in subsets(direct):
             other = tuple(1 - own[dim] if dim in flips else own[dim] for dim in C_DIMS)
             waits.append(sems.remote(here, here, g.at[other + (EVERY, columns)], across(*flips)))
         direct_waits.append(waits)
+        total = rounded.astype(F32)
+        hid[:, columns] = total
+        squares = squares + jnp.sum(total * total, axis=1, keepdims=True)
 
     ss[0] = jnp.broadcast_to(squares, (16, 128))
     square_waits = [
@@ -450,19 +445,21 @@
             target[:, :, :, :, q // 2, q % 2, :, columns] = block
 
     summed = reduce_scatter(down, ah, rh, C_DIMS, C_GROUPS, C_PIECES)
-    for columns, mine, others in summed:
+    before, waits = len(sems.pending), []
+    for columns, mine, others, last in summed:
+        for wait in last:
+            wait()
         total = hid[:, columns] + ah[mine].astype(F32)
         for other in others:
             total = total + rh[other].astype(F32)
         outs[:, columns] = total
-
-    for j in range(4):
-        fsend[j // 2, j % 2] = outs[4 * j:4 * j + 4, :]
-    before = len(sems.pending)
-    waits = [
-        sems.remote(fsend.at[p1, p0], frecv.at[x1, x0], frecv.at[p1, p0], device)
-        for device, p1, p0 in lines
-    ]
+        for j in range(4):
+            fsend[j // 2, j % 2, :, columns] = outs[4 * j:4 * j + 4, columns]
+        for device, p1, p0 in lines:
+            tail = (EVERY, columns)
+            waits.append(
+                sems.remote(fsend.at[(p1, p0) + tail], frecv.at[(x1, x0) + tail], frecv.at[(p1, p0) + tail], device)
+            )
     frecv[x1, x0] = fsend[x1, x0]
     everyone.wait_send()
     sems.drain(before)

time: 90.9 us -> 89.6 us (0.986)
  Pallas kernels: 89.2 us -> 88 us
    pallas_call x1, Pallas kernels: 89.2 us -> 88 us  [layer(): pl.pallas_call(kernel, out_shape=jax.ShapeDtypeStruct((4, D), BF), in_spe...]
where the time goes in v7:
time: 89.6 us; the launch traced here: 89.4 us
  Pallas kernels  88 us (98%)
  local copies, waits for them, and re-layouts  1.46 us (2%)
    pallas_call x1, Pallas kernels, layer(): pl.pallas_call(kernel, out_shape=jax.ShapeDtypeStruct((4, D), BF), in_spe...  88 us

profile of v7, /device:TPU:0, one launch (start us, length us, event | category | flops | bytes accessed | tf_op | source)
XLA Modules:
  0.0 89.4 jit_solution(17969430390157351623)
XLA Ops:
  0.0 88.0 %shard_map.109 = bf16[4,7168]{1,0:T(4,128)(2,1)} custom-call(s32[4]{0:T(128)} %len_ref.1, bf16[4,7168]{1,0:T(4,128)(2,1)} %res_ref.1, s32[4,8]{1,0:T(4,128)} %ids_ref.1, f32[4,8]{1,0:T(4,128)} %rw_ref.1, bf16[512,128]{1,0:T(8,128)(2,1)} %bitcast.9, bf16[4,64,576]{2,1,0:T(8,128)(2,1)} %q_hbm.1, bf16[4,576,512]{2,1,0:T(8,128)(2,1)} %bitcast.8, ...), custom_call_target="tpu_custom_call" | custom-call | tf_op jit(solution)/shard_map/pallas_call | solution.py:478
  88.0 1.5 %copy.13 = bf16[4,7168]{1,0:T(4,128)(2,1)} copy(bf16[4,7168]{1,0:T(4,128)(2,1)} %shard_map.109) | data formatting | bytes 114688
